TPU v7x, 256 devices: a whole 4x4x8 slice. The times are simulated.
256 devices in a mesh: dp: 64 (over z_hi, y, x), tensor: 4 (over z_lo, core).
Axes of the slice: x: 4, y: 4, z: 8 (z_hi: 4, z_lo: 2; z = z_hi * 2 + z_lo), core: 2. Of those that a mesh axis runs over, the one named last changes fastest.
Arguments:
- layer_input: bfloat16 [32768, 4096], P(('dp', 'tensor')), may hold values from -6 to 6
- out_grad: bfloat16 [32768, 4096], P(('dp', 'tensor')), may hold values from -6 to 6
- expert_ids: int32 [32768, 1], P(('dp', 'tensor')), may hold values from 0 to 63; in each aligned block of 128 rows (0 to 127, 128 to 255, ...) at most 3 rows name the same one
- gate_level: int32 [32768, 1], P(('dp', 'tensor')), may hold values from 1 to 8
- w_gate: bfloat16 [64, 4096, 1024], P('dp', None, 'tensor'), may hold values from -0.09375 to 0.09375
- w_up: bfloat16 [64, 4096, 1024], P('dp', None, 'tensor'), may hold values from -0.09375 to 0.09375
- w_down: bfloat16 [64, 1024, 4096], P('dp', 'tensor'), may hold values from -0.1875 to 0.1875
- attn_queries: bfloat16 [8192, 8192], P('dp', 'tensor'), may hold values from -36 to 36
- attn_keys: bfloat16 [8192, 512], P('dp', 'tensor'), may hold values from -12 to 12
- attn_values: bfloat16 [8192, 512], P('dp', 'tensor'), may hold values from -6 to 6
- attn_grad: bfloat16 [8192, 8192], P('dp', 'tensor'), may hold values from -6 to 6
Outputs:
- moe_out: bfloat16 [32768, 4096], P(('dp', 'tensor'))
- grad_x: bfloat16 [32768, 4096], P(('dp', 'tensor'))
- attn_out: bfloat16 [8192, 8192], P('dp', 'tensor')
- grad_q: bfloat16 [8192, 8192], P('dp', 'tensor')
- grad_k: bfloat16 [8192, 512], P('dp', 'tensor')
- grad_v: bfloat16 [8192, 512], P('dp', 'tensor')
Inputs may be any that keep to these rules, and one draw needn't show every extreme that they name: `expert_ids`: each row names one expert; among the rows of one device (aligned blocks of 128 rows) no expert is named more than 3 times, a bound that some block reaches.
All inputs are finite; a program needn't handle non-finite values.
Results may differ from a plain program's by a relative error of at most 0.02.
Values may be sent and summed in bfloat16 or wider, within the bound.
No kernel may reach another device: no remote copies, remote signals or barrier semaphores. Data moves between devices by JAX's collectives and lax.ppermute only.
A program may use at most 128 MiB of HBM per device.

v0:
```python
import jax
import jax.numpy as jnp
from jax import lax
from jax.sharding import PartitionSpec as P

HD = 128


def attend(queries, keys, values):
    length = queries.shape[0]
    groups = keys.shape[1] // HD
    heads = queries.shape[1] // HD
    query_f = queries.astype(jnp.float32).reshape(length, groups, heads // groups, HD)
    key_f = keys.astype(jnp.float32).reshape(length, groups, HD)
    value_f = values.astype(jnp.float32).reshape(length, groups, HD)
    scores = jnp.einsum("tgrd,ugd->grtu", query_f, key_f) * HD ** (-0.5)
    causal_mask = jnp.arange(length)[:, None] >= jnp.arange(length)[None, :]
    scores = jnp.where(causal_mask, scores, -1e30)
    top_score = jnp.max(scores, axis=-1, keepdims=True)
    raised = jnp.exp(scores - top_score)
    weights = (raised / jnp.sum(raised, axis=-1, keepdims=True)).astype(jnp.bfloat16)
    mixed = jnp.einsum("grtu,ugd->tgrd", weights.astype(jnp.float32), value_f)
    return mixed.reshape(length, heads * HD).astype(jnp.bfloat16)


def route_tables(expert_ids, gate_level, experts, capacity):
    tok_src, top_count = expert_ids.shape
    routes = tok_src * top_count
    flat_ids = expert_ids.reshape(routes)
    expert_hot = (flat_ids[:, None] == jnp.arange(experts, dtype=jnp.int32)[None, :]).astype(
        jnp.int32
    )
    slot_rank = jnp.sum((jnp.cumsum(expert_hot, axis=0) - expert_hot) * expert_hot, axis=1)
    slot_index = flat_ids * capacity + slot_rank
    slot_hot = (
        slot_index[:, None] == jnp.arange(experts * capacity, dtype=jnp.int32)[None, :]
    ).astype(jnp.float32)
    route_token = jnp.arange(routes, dtype=jnp.int32) // top_count
    token_hot = (route_token[:, None] == jnp.arange(tok_src, dtype=jnp.int32)[None, :]).astype(
        jnp.float32
    )
    gate_value = gate_level.reshape(routes).astype(jnp.float32) / 8.0
    contract = (((0,), (0,)), ((), ()))
    placing = lax.dot_general(slot_hot, token_hot, contract, preferred_element_type=jnp.float32)
    scaling = lax.dot_general(
        slot_hot, token_hot * gate_value[:, None], contract, preferred_element_type=jnp.float32
    )
    return (placing.astype(jnp.bfloat16), scaling.astype(jnp.bfloat16))


def on_device(
    layer_input,
    out_grad,
    expert_ids,
    gate_level,
    w_gate,
    w_up,
    w_down,
    attn_queries,
    attn_keys,
    attn_values,
    attn_grad,
):
    experts = lax.axis_size("dp")
    tok_src, top_count = expert_ids.shape
    capacity = max(2, tok_src * top_count // experts + 1)
    width = layer_input.shape[1]
    rows_dev = experts * capacity
    contract = (((1,), (1,)), ((), ()))
    backward = (((0,), (0,)), ((), ()))
    placing, scaling = route_tables(expert_ids, gate_level, experts, capacity)
    input_slots = jnp.dot(placing, layer_input, preferred_element_type=jnp.float32).astype(
        jnp.bfloat16
    )
    input_slots = input_slots.reshape(experts, capacity, width)
    grad_slots = jnp.dot(scaling, out_grad, preferred_element_type=jnp.float32).astype(jnp.bfloat16)
    grad_slots = grad_slots.reshape(experts, capacity, width)
    gate_w = w_gate[0]
    up_w = w_up[0]
    down_w = w_down[0]
    group_width = gate_w.shape[1]
    arrived_in = lax.all_to_all(input_slots, "dp", split_axis=0, concat_axis=0, tiled=True).reshape(
        1, rows_dev, width
    )
    shard_rows = lax.all_gather(arrived_in, "tensor", axis=0, tiled=True)
    flat_rows = shard_rows.reshape(-1, width)
    gate_part = jnp.dot(flat_rows, gate_w, preferred_element_type=jnp.float32)
    up_part = jnp.dot(flat_rows, up_w, preferred_element_type=jnp.float32)
    joined = jnp.concatenate([gate_part, up_part], axis=1)
    acts = joined.reshape(shard_rows.shape[0], shard_rows.shape[1], 2 * group_width)
    acts = acts.reshape(-1, 2 * group_width)
    gate_pre = acts[:, :group_width]
    up_pre = acts[:, group_width:]
    hidden = (gate_pre * jax.nn.sigmoid(gate_pre) * up_pre).astype(jnp.bfloat16)
    out_rows = lax.psum_scatter(
        jnp.dot(hidden, down_w, preferred_element_type=jnp.float32).astype(jnp.bfloat16),
        "tensor",
        scatter_dimension=0,
        tiled=True,
    )
    out_back = lax.all_to_all(
        out_rows.reshape(experts, capacity, width), "dp", split_axis=0, concat_axis=0, tiled=True
    )
    out_back = out_back.reshape(rows_dev, width)
    attn_out, pull = jax.vjp(attend, attn_queries, attn_keys, attn_values)
    arrived_grad = lax.all_to_all(
        grad_slots, "dp", split_axis=0, concat_axis=0, tiled=True
    ).reshape(1, rows_dev, width)
    shard_rows = lax.all_gather(arrived_grad, "tensor", axis=0, tiled=True)
    flat_rows = shard_rows.reshape(-1, width)
    result = lax.dot_general(flat_rows, down_w, contract, preferred_element_type=jnp.float32)
    d_hidden = result.reshape(shard_rows.shape[0], shard_rows.shape[1], group_width)
    d_hidden = d_hidden.reshape(-1, group_width)
    sigma = jax.nn.sigmoid(gate_pre)
    activated = gate_pre * sigma
    derivatives_d_gate = (d_hidden * up_pre * sigma * (1.0 + gate_pre * (1.0 - sigma))).astype(
        jnp.bfloat16
    )
    derivatives_d_up = (d_hidden * activated).astype(jnp.bfloat16)
    grad_q, grad_k, grad_v = pull(attn_grad)
    gate_part = derivatives_d_gate
    up_part = derivatives_d_up
    result = lax.dot_general(gate_part, gate_w, contract, preferred_element_type=jnp.float32)
    grad_rows = lax.psum_scatter(
        (
            result + lax.dot_general(up_part, up_w, contract, preferred_element_type=jnp.float32)
        ).astype(jnp.bfloat16),
        "tensor",
        scatter_dimension=0,
        tiled=True,
    )
    grad_back = lax.all_to_all(
        grad_rows.reshape(experts, capacity, width), "dp", split_axis=0, concat_axis=0, tiled=True
    )
    grad_back = grad_back.reshape(rows_dev, width)
    moe_out = lax.dot_general(
        scaling, out_back, backward, preferred_element_type=jnp.float32
    ).astype(jnp.bfloat16)
    grad_x = lax.dot_general(
        placing, grad_back, backward, preferred_element_type=jnp.float32
    ).astype(jnp.bfloat16)
    return (moe_out, grad_x, attn_out, grad_q, grad_k, grad_v)


def solution(mesh):
    in_specs = (
        P(("dp", "tensor"), None),
        P(("dp", "tensor"), None),
        P(("dp", "tensor"), None),
        P(("dp", "tensor"), None),
        P("dp", None, "tensor"),
        P("dp", None, "tensor"),
        P("dp", "tensor", None),
        P("dp", "tensor"),
        P("dp", "tensor"),
        P("dp", "tensor"),
        P("dp", "tensor"),
    )
    out_specs = (
        P(("dp", "tensor"), None),
        P(("dp", "tensor"), None),
        P("dp", "tensor"),
        P("dp", "tensor"),
        P("dp", "tensor"),
        P("dp", "tensor"),
    )
    return jax.shard_map(
        on_device, mesh=mesh, in_specs=in_specs, out_specs=out_specs, check_vma=False
    )
```

profile of v0, /device:TPU:32, one launch (start us, length us, event | category | flops | bytes accessed | tf_op | source)
XLA Modules:
  0.0 528.7 jit_solution(606218250792152010)
XLA Ops:
  7.2 0.9 fusion.44
  8.1 0.2 reduce_window_sum.11
  8.3 0.8 select_reduce_fusion
  9.1 0.7 fusion.51
  9.8 0.3 convolution_convert_fusion.8
  10.1 3.0 convolution_convert_fusion.2
  13.0 4.1 reshape.146
  17.1 66.7 %all_to_all.20 = bf16[64,3,4096]{2,1,0:T(4,128)(2,1)} all-to-all(bf16[64,3,4096]{2,1,0:T(4,128)(2,1)} %reshape.146), channel_id=1, replica_groups=mesh['dp'=64,'tensor'=4] {'dp'}, dimensions={0} | all-to-all | bytes 3145728 | tf_op jit(solution)/shard_map/all_to_all | solution.py:82
  83.9 4.4 reshape.147
  88.4 0.3 convolution_convert_fusion.9
  88.7 1.8 convolution_convert_fusion.1
  90.5 4.1 reshape.151
  94.6 79.9 %all_to_all.21 = bf16[64,3,4096]{2,1,0:T(4,128)(2,1)} all-to-all(bf16[64,3,4096]{2,1,0:T(4,128)(2,1)} %reshape.151), channel_id=1, replica_groups=mesh['dp'=64,'tensor'=4] {'dp'}, dimensions={0} | all-to-all | bytes 3145728 | tf_op jit(solution)/shard_map/all_to_all | solution.py:106
  174.5 4.3 reshape.152
  178.9 14.4 %all-gather.3.cloned.1.call-done = bf16[4,192,4096]{2,1,0:T(8,128)(2,1)} async-done(((bf16[1,192,4096]{2,1,0:T(8,128)(2,1)}), bf16[4,192,4096]{2,1,0:T(8,128)(2,1)}) %all-gather.3.cloned.1.call-update) | async-done | bytes 6291472 | tf_op jit(solution)/shard_map/all_gather | solution.py:85
  193.2 5.4 %fusion.4 = f32[768,256]{1,0:T(8,128)S(1)} fusion(bf16[768,4096]{1,0:T(8,128)(2,1)} %bitcast.132, bf16[1,4096,256]{2,1,0:T(8,128)(2,1)} %param.16), kind=kOutput, calls=%fused_computation.10 | convolution fusion | flops 1610612736 | bytes 9175040 | tf_op jit(solution)/shard_map/dot_general | solution.py:88
  198.6 0.5 copy-done.19
  199.1 1.8 fusion.8
  200.9 4.5 convolution_convert_fusion
  205.4 0.2 reduce-scatter.5.cloned.1.call-start
  205.6 56.3 %all-gather.5.cloned.1.call-done = bf16[4,192,4096]{2,1,0:T(8,128)(2,1)} async-done(((bf16[1,192,4096]{2,1,0:T(8,128)(2,1)}), bf16[4,192,4096]{2,1,0:T(8,128)(2,1)}) %all-gather.5.cloned.1.call-update) | async-done | bytes 6291472 | tf_op jit(solution)/shard_map/all_gather | solution.py:109
  262.0 4.8 fusion
  266.7 0.9 copy-done.6
  267.6 2.0 fusion.6
  269.7 5.8 %add_convert_fusion = bf16[768,4096]{1,0:T(8,128)(2,1)} fusion(f32[768,4096]{1,0:T(8,128)S(1)} %fusion.6, bf16[1,4096,256]{2,1,0:T(8,128)(2,1)S(1)} %copy-done.10, f32[768,256]{1,0:T(8,128)} %copy-done.6, f32[768,256]{1,0:T(8,128)S(1)} %fusion.8), kind=kOutput, calls=%fused_computation | convolution fusion | flops 1618083840 | bytes 22544384 | tf_op jit(solution)/shard_map/dot_general | solution.py:126
  275.4 54.5 %reduce-scatter.3.cloned.1.call-done = bf16[192,4096]{1,0:T(8,128)(2,1)} async-done(((bf16[768,4096]{1,0:T(8,128)(2,1)}), bf16[192,4096]{1,0:T(8,128)(2,1)}) %reduce-scatter.3.cloned.1.call-update) | async-done | bytes 1572880 | tf_op jit(solution)/shard_map/reduce_scatter | solution.py:95
  330.0 4.1 reshape.149
  334.1 13.7 %all-to-all-start.1 = ((bf16[64,3,4096]{2,1,0:T(4,128)(2,1)}), bf16[64,3,4096]{2,1,0:T(4,128)(2,1)S(1)}, u32[]{:S(2)}, u32[]{:S(2)}) async-start(bf16[64,3,4096]{2,1,0:T(4,128)(2,1)} %reshape.149), calls=%async_computation.2 | async-start | bytes 4194304 | tf_op jit(solution)/shard_map/all_to_all | solution.py:101
  347.8 1.0 copy.45
  348.8 94.1 %reduce-scatter.5.cloned.1.call-done = bf16[192,4096]{1,0:T(8,128)(2,1)} async-done(((bf16[768,4096]{1,0:T(8,128)(2,1)}), bf16[192,4096]{1,0:T(8,128)(2,1)}) %reduce-scatter.5.cloned.1.call-update) | async-done | bytes 1572880 | tf_op jit(solution)/shard_map/reduce_scatter | solution.py:124
  442.9 4.1 reshape.154
  447.0 14.2 %all-to-all-start.3 = ((bf16[64,3,4096]{2,1,0:T(4,128)(2,1)}), bf16[64,3,4096]{2,1,0:T(4,128)(2,1)}, u32[]{:S(2)}, u32[]{:S(2)}) async-start(bf16[64,3,4096]{2,1,0:T(4,128)(2,1)} %reshape.154), calls=%async_computation.5 | async-start | bytes 4194304 | tf_op jit(solution)/shard_map/all_to_all | solution.py:132
  461.2 1.4 fusion.63
  462.6 0.2 fusion.23
  462.8 0.4 fusion.19
  463.2 0.6 fusion.62
  463.8 0.8 copy-done.3
  464.6 1.1 convolution_convert_fusion.7
  465.8 2.0 copy.39
  467.8 2.5 convolution_convert_fusion.5
  470.4 2.1 copy.40
  472.4 2.1 fusion.12
  474.6 2.4 fusion.13
  477.0 2.5 reshape.150
  479.5 2.8 convolution_convert_fusion.4
  482.4 32.5 %all-to-all-done.3 = bf16[64,3,4096]{2,1,0:T(4,128)(2,1)} async-done(((bf16[64,3,4096]{2,1,0:T(4,128)(2,1)}), bf16[64,3,4096]{2,1,0:T(4,128)(2,1)}, u32[]{:S(2)}, u32[]{:S(2)}) %all-to-all-start.3) | async-done | bytes 1572896 | tf_op jit(solution)/shard_map/all_to_all | solution.py:132
  514.9 4.4 reshape.155
  519.3 2.8 convolution_convert_fusion.3
  (52 shorter events, 0.3 us)
Async XLA Ops:
  7.2 193.7 %copy-start = (bf16[1,256,4096]{2,1,0:T(8,128)(2,1)S(1)}, bf16[1,256,4096]{2,1,0:T(8,128)(2,1)}, u32[]{:S(2)}) copy-start(bf16[1,256,4096]{2,1,0:T(8,128)(2,1)} %param.17) | copy-start | bytes 6291460
  7.2 186.0 %all-gather.3.cloned.1.call-start = ((), (), s32[]{:S(2)}) async-start(), calls=%async_computation.6 | async-start | bytes 7864320 | tf_op jit(solution)/shard_map/all_gather | solution.py:85
  83.9 4.5 copy-start.20
  83.9 4.8 copy-start.11
  88.3 173.6 %all-gather.5.cloned.1.call-start = ((), (), s32[]{:S(2)}) async-start(), calls=%async_computation.8 | async-start | bytes 7864320 | tf_op jit(solution)/shard_map/all_gather | solution.py:109
  178.8 151.2 %reduce-scatter.3.cloned.1.call-start = ((), (), s32[]{:S(2)}) async-start(), calls=%async_computation.7 | async-start | bytes 7864320 | tf_op jit(solution)/shard_map/reduce_scatter | solution.py:95
  193.2 5.4 %copy-start.8 = (bf16[1,4096,256]{2,1,0:T(8,128)(2,1)S(1)}, bf16[1,4096,256]{2,1,0:T(8,128)(2,1)}, u32[]{:S(2)}) copy-start(bf16[1,4096,256]{2,1,0:T(8,128)(2,1)} %param.15) | copy-start | bytes 6291460
  193.2 5.8 %copy-start.19 = (bf16[4,192,4096]{2,1,0:T(8,128)(2,1)S(1)}, bf16[4,192,4096]{2,1,0:T(8,128)(2,1)}, u32[]{:S(2)}) copy-start(bf16[4,192,4096]{2,1,0:T(8,128)(2,1)} %all-gather.3.cloned.1.call-done) | copy-start | bytes 18874372
  199.0 1.8 copy-start.4
  205.4 237.5 %reduce-scatter.5.cloned.1.call-start = ((), (), s32[]{:S(2)}) async-start(), calls=%async_computation.9 | async-start | bytes 7864320 | tf_op jit(solution)/shard_map/reduce_scatter | solution.py:124
  261.9 5.7 %copy-start.5 = (f32[768,256]{1,0:T(8,128)S(1)}, f32[768,256]{1,0:T(8,128)}, u32[]{:S(2)}) copy-start(f32[768,256]{1,0:T(8,128)} %copy-done.4) | copy-start | bytes 2359300
  262.0 5.7 %copy-start.9 = (bf16[1,4096,256]{2,1,0:T(8,128)(2,1)S(1)}, bf16[1,4096,256]{2,1,0:T(8,128)(2,1)}, u32[]{:S(2)}) copy-start(bf16[1,4096,256]{2,1,0:T(8,128)(2,1)} %param.15) | copy-start | bytes 6291460
  266.7 0.9 copy-start.6
  267.6 2.0 copy-start.10
  334.1 13.7 %copy-start.12 = (bf16[128,2048]{1,0:T(8,128)(2,1)S(1)}, bf16[128,2048]{1,0:T(8,128)(2,1)}, u32[]{:S(2)}) copy-start(bf16[128,2048]{1,0:T(8,128)(2,1)} %param.21) | copy-start | bytes 1572868
  334.1 112.9 %all-to-all-start.1 = ((bf16[64,3,4096]{2,1,0:T(4,128)(2,1)}), bf16[64,3,4096]{2,1,0:T(4,128)(2,1)S(1)}, u32[]{:S(2)}, u32[]{:S(2)}) async-start(bf16[64,3,4096]{2,1,0:T(4,128)(2,1)} %reshape.149), calls=%async_computation.2 | async-start | bytes 4194304 | tf_op jit(solution)/shard_map/all_to_all | solution.py:101
  446.9 14.2 %copy-start.16 = (bf16[128,128]{1,0:T(8,128)(2,1)S(1)}, bf16[128,128]{1,0:T(8,128)(2,1)}, u32[]{:S(2)}) copy-start(bf16[128,128]{1,0:T(8,128)(2,1)} %param.19) | copy-start | bytes 98308
  447.0 67.9 %all-to-all-start.3 = ((bf16[64,3,4096]{2,1,0:T(4,128)(2,1)}), bf16[64,3,4096]{2,1,0:T(4,128)(2,1)}, u32[]{:S(2)}, u32[]{:S(2)}) async-start(bf16[64,3,4096]{2,1,0:T(4,128)(2,1)} %reshape.154), calls=%async_computation.5 | async-start | bytes 4194304 | tf_op jit(solution)/shard_map/all_to_all | solution.py:132
  461.1 1.7 copy-start.2
  461.1 1.7 copy-start.13
  463.2 2.6 copy-start.7
  463.2 2.6 copy-start.14
  463.8 0.8 copy-start.3
  467.8 2.6 copy-start.17
  470.4 4.2 copy-start.15
  470.4 4.2 copy-start.18
  514.9 7.3 %copy-start.1 = (bf16[1,256,4096]{2,1,0:T(8,128)(2,1)S(1)}, bf16[1,256,4096]{2,1,0:T(8,128)(2,1)}, u32[]{:S(2)}) copy-start(bf16[1,256,4096]{2,1,0:T(8,128)(2,1)} %param.17) | copy-start | bytes 6291460
Sparse Core Ops, SparseCore 0:
  88.4 104.7 all-gather.2
  195.0 66.8 all-gather.4
  264.5 65.4 reduce-scatter.2
  332.4 110.4 reduce-scatter.4
where the time goes:
time: 530 us; the launch traced here: 529 us
  waiting for transfers between devices  252 us (48%)
  blocking collectives  147 us (28%)
  matrix products  45.2 us (9%)
  local copies, waits for them, and re-layouts  39.3 us (7%)
  starting transfers between devices  28.2 us (5%)
  between operations  14.1 us (3%)
    reduce_scatter x1, waiting for transfers between devices, on_device(): lax.psum_scatter((result + lax.dot_general(up_part, up_w, contract, prefe...  94.1 us
    all_to_all x1, blocking collectives, on_device(): lax.all_to_all(grad_slots, 'dp', split_axis=0, concat_axis=0, tiled=True)  79.9 us
    all_to_all x1, blocking collectives, on_device(): lax.all_to_all(input_slots, 'dp', split_axis=0, concat_axis=0, tiled=True)  66.7 us
    all_gather x1, waiting for transfers between devices, on_device(): shard_rows = lax.all_gather(arrived_grad, 'tensor', axis=0, tiled=True)  56.3 us
    reduce_scatter x1, waiting for transfers between devices, on_device(): lax.psum_scatter(jnp.dot(hidden, down_w, preferred_element_type=jnp.float...  54.5 us
    all_to_all x1, waiting for transfers between devices, on_device(): lax.all_to_all(grad_rows.reshape(experts, capacity, width), 'dp', split_a...  32.5 us
    all_gather x1, waiting for transfers between devices, on_device(): shard_rows = lax.all_gather(arrived_in, 'tensor', axis=0, tiled=True)  14.4 us
    all_to_all x1, starting transfers between devices, on_device(): lax.all_to_all(grad_rows.reshape(experts, capacity, width), 'dp', split_a...  14.2 us
  transfers between devices with their start and end apart: 6, of which 5 were waited for; matrix products, arithmetic and copies ran while one was open for 12% of the time, Pallas kernels for 0%

commit v1 on v0

v1 whole, which is shorter than its diff:
```python
import functools

import jax
import jax.numpy as jnp
import numpy as np
from jax import lax
from jax.experimental import pallas as pl
from jax.experimental.pallas import tpu as pltpu
from jax.sharding import PartitionSpec as P

HD = 128
AXES = ("dp", "tensor")
SLOTS = 3
QUARTERS = 4
BLK = 48
VMEM_LIMIT = 40 * 1024 * 1024
BF = jnp.bfloat16
F32 = jnp.float32
NT = (((1,), (1,)), ((), ()))
TN = (((0,), (0,)), ((), ()))


def linear(x, y, z, core):
    return ((z // 2) * 16 + y * 4 + x) * 4 + (z % 2) * 2 + core


def moves(target):
    pairs = []
    for x in range(4):
        for y in range(4):
            for z in range(8):
                for core in range(2):
                    z_to, core_to = target(z, core)
                    pairs.append((linear(x, y, z, core), linear(x, y, z_to % 8, core_to)))
    return pairs


INNER = moves(lambda z, c: (z ^ 1, c))
CORES = moves(lambda z, c: (z, 1 - c))
NEAR = [
    moves(lambda z, c: (z - 2 if z % 2 else z + 2, c)),
    moves(lambda z, c: (z + 3 if z % 2 else z - 3, c)),
    moves(lambda z, c: (z + 1 if z % 2 else z - 1, c)),
]
BACK = [[(b, a) for a, b in perm] for perm in NEAR]
PLANES = [
    [linear(x, y, z, c) for y in range(4) for x in range(4)] for z in range(8) for c in range(2)
]


def send(value, perm):
    return lax.ppermute(value, AXES, perm)


def plane_exchange(value):
    return lax.all_to_all(value, AXES, 0, 0, axis_index_groups=PLANES, tiled=True)


def params(**more):
    return pltpu.CompilerParams(vmem_limit_bytes=VMEM_LIMIT, **more)


def cost(flops, nbytes):
    return pl.CostEstimate(flops=flops, bytes_accessed=nbytes, transcendentals=0)


def first_row(ids, rank, where):
    pair, odd = where[0], where[1]
    turn = ((ids >> 4) - pair) & 3
    turn = jnp.where(odd == 1, (4 - turn) & 3, turn)
    return (ids & 15) * BLK + turn * SLOTS + rank


def dispatch_kernel(where, ids_row, ids_col, level_row, x_ref, out_ref, *, scaled):
    tokens = ids_row.shape[1]
    ids = ids_row[...]
    earlier = lax.broadcasted_iota(jnp.int32, (tokens, tokens), 0) < lax.broadcasted_iota(
        jnp.int32, (tokens, tokens), 1
    )
    same = jnp.where(earlier & (ids_col[...] == ids), 1, 0)
    rank = jnp.sum(same, axis=0, keepdims=True)
    base = first_row(ids, rank, where)
    rows = out_ref.shape[0]
    width = out_ref.shape[1]
    row = lax.broadcasted_iota(jnp.int32, (rows, tokens), 0)
    if scaled:
        value = jnp.broadcast_to(level_row[...].astype(F32) * 0.125, (rows, tokens))
    else:
        value = jnp.full((rows, tokens), 1.0, F32)
    total = jnp.zeros((rows, width), F32)
    for q in range(QUARTERS):
        hot = jnp.where(row == base + q * (4 * SLOTS), value, 0.0).astype(BF)
        total = total + jnp.dot(
            hot, x_ref[:, q * width : (q + 1) * width], preferred_element_type=F32
        )
    out_ref[...] = total.astype(BF)


def dispatch(where, ids_row, ids_col, level_row, x, scaled):
    tokens, d = x.shape
    rows, width = 16 * BLK, d // QUARTERS
    vmem = pl.BlockSpec(memory_space=pltpu.VMEM)
    out = pl.pallas_call(
        functools.partial(dispatch_kernel, scaled=scaled),
        out_shape=jax.ShapeDtypeStruct((rows, width), BF),
        in_specs=[pl.BlockSpec(memory_space=pltpu.SMEM), vmem, vmem, vmem, vmem],
        out_specs=vmem,
        compiler_params=params(),
        cost_estimate=cost(2 * rows * tokens * d, 4 * rows * width),
        name="dispatch",
    )(where, ids_row, ids_col, level_row, x)
    return out.reshape(16, BLK, width)


def combine_kernel(where, ids_row, ids_col, level_col, back_ref, out_ref, *, scaled):
    q = pl.program_id(0)
    tokens = ids_row.shape[1]
    ids = ids_col[...]
    earlier = lax.broadcasted_iota(jnp.int32, (tokens, tokens), 1) < lax.broadcasted_iota(
        jnp.int32, (tokens, tokens), 0
    )
    same = jnp.where(earlier & (ids == ids_row[...]), 1, 0)
    rank = jnp.sum(same, axis=1, keepdims=True)
    base = first_row(ids, rank, where) + q * (4 * SLOTS)
    rows = back_ref.shape[0]
    row = lax.broadcasted_iota(jnp.int32, (tokens, rows), 1)
    if scaled:
        value = jnp.broadcast_to(level_col[...].astype(F32) * 0.125, (tokens, rows))
    else:
        value = jnp.full((tokens, rows), 1.0, F32)
    hot = jnp.where(row == base, value, 0.0).astype(BF)
    out_ref[...] = jnp.dot(hot, back_ref[...], preferred_element_type=F32).astype(BF)


def combine(where, ids_row, ids_col, level_col, back, scaled):
    back = back.reshape(-1, back.shape[-1])
    rows, width = back.shape
    tokens = ids_row.shape[1]
    fixed = lambda q: (0, 0)
    return pl.pallas_call(
        functools.partial(combine_kernel, scaled=scaled),
        out_shape=jax.ShapeDtypeStruct((tokens, QUARTERS * width), BF),
        grid=(QUARTERS,),
        in_specs=[
            pl.BlockSpec(memory_space=pltpu.SMEM),
            pl.BlockSpec((1, tokens), fixed),
            pl.BlockSpec((tokens, 1), fixed),
            pl.BlockSpec((tokens, 1), fixed),
            pl.BlockSpec((rows, width), fixed),
        ],
        out_specs=pl.BlockSpec((tokens, width), lambda q: (0, q)),
        compiler_params=params(),
        cost_estimate=cost(2 * rows * tokens * width * QUARTERS, 4 * rows * width),
        name="combine",
    )(where, ids_row, ids_col, level_col, back)


def shuffle_matrix():
    source, q, turn, slot = np.meshgrid(
        np.arange(16), np.arange(4), np.arange(4), np.arange(SLOTS), indexing="ij"
    )
    by_source = source * BLK + q * 12 + turn * SLOTS + slot
    by_turn = turn * 192 + q * BLK + source * SLOTS + slot
    matrix = np.zeros((768, 768), np.float32)
    matrix[by_turn.ravel(), by_source.ravel()] = 1.0
    return matrix


def shuffle_kernel(matrix, rows_ref, *outs):
    for turn, out in enumerate(outs):
        part = jnp.dot(
            matrix[turn * 192 : (turn + 1) * 192, :], rows_ref[...], preferred_element_type=F32
        )
        out[...] = part.astype(BF).reshape(out.shape)


def shuffle(rows):
    width = rows.shape[-1]
    flat = rows.reshape(768, width)
    vmem = pl.BlockSpec(memory_space=pltpu.VMEM)
    return pl.pallas_call(
        shuffle_kernel,
        out_shape=[jax.ShapeDtypeStruct((QUARTERS, BLK, width), BF)] * 4,
        in_specs=[vmem, vmem],
        out_specs=[vmem] * 4,
        compiler_params=params(),
        cost_estimate=cost(2 * 768 * 768 * width, 4 * 768 * width),
        name="shuffle",
    )(jnp.asarray(shuffle_matrix(), BF), flat)


def unshuffle_kernel(matrix, b0, b1, b2, b3, out_ref):
    total = None
    for turn, block in enumerate((b0, b1, b2, b3)):
        flat = block[...].reshape(192, block.shape[-1])
        part = jnp.dot(
            matrix[:, turn * 192 : (turn + 1) * 192], flat, preferred_element_type=F32
        )
        total = part if total is None else total + part
    out_ref[...] = total.astype(BF)


def unshuffle(blocks):
    width = blocks[0].shape[-1]
    vmem = pl.BlockSpec(memory_space=pltpu.VMEM)
    out = pl.pallas_call(
        unshuffle_kernel,
        out_shape=jax.ShapeDtypeStruct((768, width), BF),
        in_specs=[vmem] * 5,
        out_specs=vmem,
        compiler_params=params(),
        cost_estimate=cost(2 * 768 * 768 * width, 4 * 768 * width),
        name="unshuffle",
    )(jnp.asarray(shuffle_matrix().T, BF), *blocks)
    return out.reshape(16, BLK, width)


def gather_rows(blocks, rows):
    for i, block in enumerate(blocks):
        rows[i * BLK : (i + 1) * BLK, :] = block[0]


def store_rows(value, near, far):
    half = value.shape[0] // 2
    near[...] = value[:half].astype(BF).reshape(near.shape)
    far[...] = value[half:].astype(BF).reshape(far.shape)


def forward_kernel(*refs):
    blocks, (wg0, wg1, wu0, wu1, wd0, wd1, near, far, acts, rows, hidden) = refs[:8], refs[8:]
    step = pl.program_id(0)
    ff = wg0.shape[1]

    @pl.when(step < QUARTERS)
    def _():
        gather_rows(blocks, rows)
        for i, w in enumerate((wg0, wg1, wu0, wu1)):
            part = jnp.dot(rows[...], w[...], preferred_element_type=F32)
            cols = slice(i * ff, (i + 1) * ff)

            @pl.when(step == 0)
            def _():
                acts[:, cols] = part

            @pl.when(step > 0)
            def _():
                acts[:, cols] = acts[:, cols] + part

    @pl.when(step == QUARTERS)
    def _():
        gate = acts[:, : 2 * ff]
        hidden[...] = (gate * jax.nn.sigmoid(gate) * acts[:, 2 * ff :]).astype(BF)

    @pl.when(step >= QUARTERS)
    def _():
        value = jnp.dot(hidden[:, :ff], wd0[...], preferred_element_type=F32)
        value = value + jnp.dot(hidden[:, ff:], wd1[...], preferred_element_type=F32)
        store_rows(value, near, far)


def backward_kernel(*refs):
    blocks, (acts, wg0, wg1, wu0, wu1, wd0, wd1, near, far, rows, dh, dacts) = refs[:8], refs[8:]
    step = pl.program_id(0)
    ff = wg0.shape[1]

    @pl.when(step < QUARTERS)
    def _():
        gather_rows(blocks, rows)
        for i, w in enumerate((wd0, wd1)):
            part = lax.dot_general(rows[...], w[...], NT, preferred_element_type=F32)
            cols = slice(i * ff, (i + 1) * ff)

            @pl.when(step == 0)
            def _():
                dh[:, cols] = part

            @pl.when(step > 0)
            def _():
                dh[:, cols] = dh[:, cols] + part

    @pl.when(step == QUARTERS)
    def _():
        gate = acts[:, : 2 * ff]
        sigma = jax.nn.sigmoid(gate)
        d_hidden = dh[...]
        d_gate = d_hidden * acts[:, 2 * ff :] * sigma * (1.0 + gate * (1.0 - sigma))
        dacts[:, : 2 * ff] = d_gate.astype(BF)
        dacts[:, 2 * ff :] = (d_hidden * (gate * sigma)).astype(BF)

    @pl.when(step >= QUARTERS)
    def _():
        value = None
        for i, w in enumerate((wg0, wg1, wu0, wu1)):
            part = lax.dot_general(
                dacts[:, i * ff : (i + 1) * ff], w[...], NT, preferred_element_type=F32
            )
            value = part if value is None else value + part
        store_rows(value, near, far)


def first_pass(step):
    return jnp.minimum(step, QUARTERS - 1)


def second_pass(step):
    return jnp.maximum(step - QUARTERS, 0)


def expert_call(kernel, blocks, acts, weights, backward):
    wg, wu, wd = weights
    width = blocks[0].shape[-1]
    ff = wg[0].shape[1]
    rows = 8 * BLK
    up_pass, down_pass = (second_pass, first_pass) if backward else (first_pass, second_pass)
    row_spec = pl.BlockSpec((1, BLK, width), lambda s: (first_pass(s), 0, 0))
    up_spec = pl.BlockSpec((width, ff), lambda s: (up_pass(s), 0))
    down_spec = pl.BlockSpec((ff, width), lambda s: (0, down_pass(s)))
    act_spec = pl.BlockSpec((rows, 4 * ff), lambda s: (0, 0))
    out_spec = pl.BlockSpec((4, 1, BLK, width), lambda s: (0, second_pass(s), 0, 0))
    out_type = jax.ShapeDtypeStruct((4, QUARTERS, BLK, width), BF)
    act_type = jax.ShapeDtypeStruct((rows, 4 * ff), F32)
    in_specs = [row_spec] * 8 + ([act_spec] if backward else []) + [up_spec] * 4 + [down_spec] * 2
    scratch = [pltpu.VMEM((rows, width), BF)]
    if backward:
        scratch += [pltpu.VMEM((rows, 2 * ff), F32), pltpu.VMEM((rows, 4 * ff), BF)]
    else:
        scratch += [pltpu.VMEM((rows, 2 * ff), BF)]
    return pl.pallas_call(
        kernel,
        out_shape=[out_type, out_type] + ([] if backward else [act_type]),
        grid=(2 * QUARTERS,),
        in_specs=in_specs,
        out_specs=[out_spec, out_spec] + ([] if backward else [act_spec]),
        scratch_shapes=scratch,
        compiler_params=params(dimension_semantics=("arbitrary",)),
        cost_estimate=cost(12 * rows * width * QUARTERS * ff, 20 * 1024 * 1024),
        name="expert_backward" if backward else "expert_forward",
    )(*blocks, *([acts] if backward else []), *wg, *wu, *wd)


HEADS_STEP = 4


def attention_kernel(q_ref, k_ref, v_ref, do_ref, o_ref, dq_ref, dk_ref, dv_ref, dk_acc, dv_acc):
    step = pl.program_id(0)
    length = k_ref.shape[0]
    scale = HD ** (-0.5)
    k = k_ref[...]
    v = v_ref[...]
    causal = lax.broadcasted_iota(jnp.int32, (length, length), 0) >= lax.broadcasted_iota(
        jnp.int32, (length, length), 1
    )
    dk = None
    dv = None
    for h in range(HEADS_STEP):
        cols = slice(h * HD, (h + 1) * HD)
        q = q_ref[:, cols]
        do = do_ref[:, cols]
        scores = lax.dot_general(q, k, NT, preferred_element_type=F32) * scale
        scores = jnp.where(causal, scores, -1e30)
        raised = jnp.exp(scores - jnp.max(scores, axis=1, keepdims=True))
        probs = raised / jnp.sum(raised, axis=1, keepdims=True)
        rounded = probs.astype(BF)
        o_ref[:, cols] = jnp.dot(rounded, v, preferred_element_type=F32).astype(BF)
        d_probs = lax.dot_general(do, v, NT, preferred_element_type=F32).astype(BF).astype(F32)
        inner = jnp.sum(d_probs * probs, axis=1, keepdims=True)
        d_scores = (probs * (d_probs - inner) * scale).astype(BF)
        dq_ref[:, cols] = jnp.dot(d_scores, k, preferred_element_type=F32).astype(BF)
        dk_part = lax.dot_general(d_scores, q, TN, preferred_element_type=F32)
        dv_part = lax.dot_general(rounded, do, TN, preferred_element_type=F32)
        dk = dk_part if dk is None else dk + dk_part
        dv = dv_part if dv is None else dv + dv_part

    @pl.when(step == 0)
    def _():
        dk_acc[...] = dk
        dv_acc[...] = dv

    @pl.when(step > 0)
    def _():
        dk_acc[...] = dk_acc[...] + dk
        dv_acc[...] = dv_acc[...] + dv

    @pl.when(step == pl.num_programs(0) - 1)
    def _():
        dk_ref[...] = dk_acc[...].astype(BF)
        dv_ref[...] = dv_acc[...].astype(BF)


def attention(queries, keys, values, cotangent):
    length, wide = queries.shape
    head_spec = pl.BlockSpec((length, HEADS_STEP * HD), lambda s: (0, s))
    key_spec = pl.BlockSpec((length, HD), lambda s: (0, 0))
    heads = wide // HD
    return pl.pallas_call(
        attention_kernel,
        out_shape=[
            jax.ShapeDtypeStruct(queries.shape, BF),
            jax.ShapeDtypeStruct(queries.shape, BF),
            jax.ShapeDtypeStruct(keys.shape, BF),
            jax.ShapeDtypeStruct(values.shape, BF),
        ],
        grid=(heads // HEADS_STEP,),
        in_specs=[head_spec, key_spec, key_spec, head_spec],
        out_specs=[head_spec, head_spec, key_spec, key_spec],
        scratch_shapes=[pltpu.VMEM((length, HD), F32)] * 2,
        compiler_params=params(dimension_semantics=("arbitrary",)),
        cost_estimate=cost(14 * heads * length * length * HD, 10 * 1024 * 1024),
        name="attention",
    )(queries, keys, values, cotangent)


def spread(rows):
    own, *others = shuffle(rows)
    near = [own] + [send(block, perm) for block, perm in zip(others, NEAR)]
    far = [send(block, INNER) for block in near]
    return near + far


def collect(near, far):
    total = (near.astype(F32) + send(far, INNER).astype(F32)).astype(BF)
    blocks = [total[0]] + [send(total[i + 1], perm) for i, perm in enumerate(BACK)]
    return plane_exchange(unshuffle(blocks))


def on_device(
    layer_input,
    out_grad,
    expert_ids,
    gate_level,
    w_gate,
    w_up,
    w_down,
    attn_queries,
    attn_keys,
    attn_values,
    attn_grad,
):
    tokens = layer_input.shape[0]
    where = jnp.stack([lax.axis_index("dp") // 16, lax.axis_index("tensor") // 2]).astype(jnp.int32)
    ids_row = expert_ids.reshape(1, tokens)
    ids_col = expert_ids.reshape(tokens, 1)
    level_row = gate_level.reshape(1, tokens)
    level_col = gate_level.reshape(tokens, 1)

    weights = [(w[0], send(w[0], CORES)) for w in (w_gate, w_up, w_down)]

    x_rows = plane_exchange(dispatch(where, ids_row, ids_col, level_row, layer_input, False))
    x_blocks = spread(x_rows)
    g_rows = plane_exchange(dispatch(where, ids_row, ids_col, level_row, out_grad, True))
    g_blocks = spread(g_rows)

    attn_out, grad_q, grad_k, grad_v = attention(attn_queries, attn_keys, attn_values, attn_grad)

    out_near, out_far, acts = expert_call(forward_kernel, x_blocks, None, weights, False)
    out_back = collect(out_near, out_far)
    grad_near, grad_far = expert_call(backward_kernel, g_blocks, acts, weights, True)
    grad_back = collect(grad_near, grad_far)

    moe_out = combine(where, ids_row, ids_col, level_col, out_back, True)
    grad_x = combine(where, ids_row, ids_col, level_col, grad_back, False)
    return (moe_out, grad_x, attn_out, grad_q, grad_k, grad_v)


def solution(mesh):
    in_specs = (
        P(("dp", "tensor"), None),
        P(("dp", "tensor"), None),
        P(("dp", "tensor"), None),
        P(("dp", "tensor"), None),
        P("dp", None, "tensor"),
        P("dp", None, "tensor"),
        P("dp", "tensor", None),
        P("dp", "tensor"),
        P("dp", "tensor"),
        P("dp", "tensor"),
        P("dp", "tensor"),
    )
    out_specs = (
        P(("dp", "tensor"), None),
        P(("dp", "tensor"), None),
        P("dp", "tensor"),
        P("dp", "tensor"),
        P("dp", "tensor"),
        P("dp", "tensor"),
    )
    return jax.shard_map(
        on_device, mesh=mesh, in_specs=in_specs, out_specs=out_specs, check_vma=False
    )
```

time: 530 us -> 356 us (0.67)
  blocking collectives: 147 us -> 0 us
  Pallas kernels: 0 us -> 63.8 us
  waiting for transfers between devices: 252 us -> 205 us
  matrix products: 45.2 us -> 0 us
  starting transfers between devices: 28.2 us -> 61.7 us
  local copies, waits for them, and re-layouts: 39.3 us -> 18.9 us
  between operations: 14.1 us -> 0.86 us
    ppermute x0 -> x25, waiting for transfers between devices: none -> 178 us  [send(): return lax.ppermute(value, AXES, perm)]
    reduce_scatter x2 -> x0, waiting for transfers between devices: 149 us -> none  [the longest x1 94.1 us: on_device(): lax.psum_scatter((result + lax.dot_general(up_part, up_w, contract, prefe...]
    all_to_all x2 -> x0, blocking collectives: 147 us -> none  [the longest x1 79.9 us: on_device(): lax.all_to_all(grad_slots, 'dp', split_axis=0, concat_axis=0, tiled=True)]
    all_gather x2 -> x0, waiting for transfers between devices: 70.7 us -> none  [the longest x1 56.3 us: on_device(): shard_rows = lax.all_gather(arrived_grad, 'tensor', axis=0, tiled=True)]
    pallas_call x0 -> x11, Pallas kernels: none -> 63.8 us  [the longest x2 28.5 us: expert_call(): pl.pallas_call(kernel, out_shape=[out_type, out_type] + ([] if backward e...]
    dot_general x18 -> x0, matrix products: 45.2 us -> none  [the longest x3 6.4 us: attend(): scores = jnp.einsum('tgrd,ugd->grtu', query_f, key_f) * HD ** (-0.5)]
    ppermute x0 -> x25, starting transfers between devices: none -> 40.7 us  [send(): return lax.ppermute(value, AXES, perm)]
    reshape x9 -> x0, local copies, waits for them, and re-layouts: 33 us -> none  [the longest x1 4.43 us: on_device(): grad_back = grad_back.reshape(rows_dev, width)]
  transfers between devices with their start and end apart: 6 -> 29, of which waited for: 5 -> 21; matrix products, arithmetic and copies ran while one was open for 12% -> 1% of each run, Pallas kernels for 0% -> 16%
where the time goes in v1:
time: 356 us; the launch traced here: 355 us
  waiting for transfers between devices  205 us (58%)
  Pallas kernels  63.8 us (18%)
  starting transfers between devices  61.7 us (17%)
  local copies, waits for them, and re-layouts  18.9 us (5%)
  other arithmetic  4.26 us (1%)
    ppermute x25, waiting for transfers between devices, send(): return lax.ppermute(value, AXES, perm)  178 us
    ppermute x25, starting transfers between devices, send(): return lax.ppermute(value, AXES, perm)  40.7 us
    pallas_call x2, Pallas kernels, expert_call(): pl.pallas_call(kernel, out_shape=[out_type, out_type] + ([] if backward e...  28.5 us
    all_to_all x4, waiting for transfers between devices, plane_exchange(): lax.all_to_all(value, AXES, 0, 0, axis_index_groups=PLANES, tiled=True)  27.5 us
    all_to_all x4, starting transfers between devices, plane_exchange(): lax.all_to_all(value, AXES, 0, 0, axis_index_groups=PLANES, tiled=True)  20.9 us
    unnamed x64, local copies, waits for them, and re-layouts  18.6 us
    pallas_call x1, Pallas kernels, attention(): pl.pallas_call(attention_kernel, out_shape=[jax.ShapeDtypeStruct(queries....  11.3 us
    pallas_call x2, Pallas kernels, combine(): pl.pallas_call(functools.partial(combine_kernel, scaled=scaled), out_shap...  7.44 us
  transfers between devices with their start and end apart: 29, of which 21 were waited for; matrix products, arithmetic and copies ran while one was open for 1% of the time, Pallas kernels for 16%

profile of v1, /device:TPU:32, one launch (start us, length us, event | category | flops | bytes accessed | tf_op | source)
XLA Modules:
  0.0 355.0 jit_solution(7060032202425091741)
XLA Ops:
  4.0 3.6 %dispatch.2 = bf16[768,1024]{1,0:T(8,128)(2,1)} custom-call(s32[2]{0:T(128)S(1)} %pad_add_fusion.where, s32[1,128]{1,0:T(1,128)S(1)} %bitcast.37, s32[128,1]{1,0:T(8,128)S(1)} %copy.22.ids_col, s32[1,128]{1,0:T(1,128)S(1)} %bitcast.35, bf16[128,4096]{1,0:T(8,128)(2,1)S(1)} %copy-done.10), custom_call_target="tpu_custom_call" | custom-call | flops 805306368 | bytes 3145728 | tf_op jit(solution)/shard_map/dispatch/pallas_call | solution.py:103
  7.7 7.2 %all-to-all-start = ((bf16[16,48,1024]{2,1,0:T(8,128)(2,1)}), bf16[16,48,1024]{2,1,0:T(8,128)(2,1)S(1)}, u32[]{:S(2)}, u32[]{:S(2)}) async-start(bf16[16,48,1024]{2,1,0:T(8,128)(2,1)} %bitcast.4), calls=%async_computation | async-start | bytes 3145728 | tf_op jit(solution)/shard_map/all_to_all | solution.py:56
  15.6 23.8 %all-to-all-done = bf16[16,48,1024]{2,1,0:T(8,128)(2,1)S(1)} async-done(((bf16[16,48,1024]{2,1,0:T(8,128)(2,1)}), bf16[16,48,1024]{2,1,0:T(8,128)(2,1)S(1)}, u32[]{:S(2)}, u32[]{:S(2)}) %all-to-all-start) | async-done | bytes 1572896 | tf_op jit(solution)/shard_map/all_to_all | solution.py:56
  39.3 1.8 shuffle.2
  42.7 5.4 %collective-permute-start = (bf16[4,48,1024]{2,1,0:T(8,128)(2,1)}, bf16[4,48,1024]{2,1,0:T(8,128)(2,1)S(1)}, u32[]{:S(2)}, u32[]{:S(2)}) collective-permute-start(bf16[4,48,1024]{2,1,0:T(8,128)(2,1)} %get-tuple-element.24), channel_id=1, source_target_pairs={{0,64},{1,65},{2,194},{3,195},{64,128},{65,129},{66,2},{67,3},{128... | collective-permute-start | bytes 1179656 | tf_op jit(solution)/shard_map/ppermute | solution.py:52
  48.1 1.9 collective-permute-start.1
  50.0 3.5 dispatch.3
  53.6 3.8 %all-to-all-start.2 = ((bf16[16,48,1024]{2,1,0:T(8,128)(2,1)}), bf16[16,48,1024]{2,1,0:T(8,128)(2,1)S(1)}, u32[]{:S(2)}, u32[]{:S(2)}) async-start(bf16[16,48,1024]{2,1,0:T(8,128)(2,1)} %bitcast.15), calls=%async_computation.2 | async-start | bytes 3145728 | tf_op jit(solution)/shard_map/all_to_all | solution.py:56
  57.4 6.0 %collective-permute-done.refs_1_ = bf16[4,48,1024]{2,1,0:T(8,128)(2,1)S(1)} collective-permute-done((bf16[4,48,1024]{2,1,0:T(8,128)(2,1)}, bf16[4,48,1024]{2,1,0:T(8,128)(2,1)S(1)}, u32[]{:S(2)}, u32[]{:S(2)}) %collective-permute-start) | collective-permute-done | bytes 393248 | tf_op jit(solution)/shard_map/ppermute | solution.py:52
  64.4 9.3 %collective-permute-done.1.refs_2_ = bf16[4,48,1024]{2,1,0:T(8,128)(2,1)S(1)} collective-permute-done((bf16[4,48,1024]{2,1,0:T(8,128)(2,1)}, bf16[4,48,1024]{2,1,0:T(8,128)(2,1)S(1)}, u32[]{:S(2)}, u32[]{:S(2)}) %collective-permute-start.1) | collective-permute-done | bytes 393248 | tf_op jit(solution)/shard_map/ppermute | solution.py:52
  73.7 5.1 %collective-permute-done.2.refs_3_ = bf16[4,48,1024]{2,1,0:T(8,128)(2,1)S(1)} collective-permute-done((bf16[4,48,1024]{2,1,0:T(8,128)(2,1)S(1)}, bf16[4,48,1024]{2,1,0:T(8,128)(2,1)S(1)}, u32[]{:S(2)}, u32[]{:S(2)}) %collective-permute-start.2) | collective-permute-done | bytes 393248 | tf_op jit(solution)/shard_map/ppermute | solution.py:52
  78.8 3.0 collective-permute-start.4
  82.6 3.1 collective-permute-done.3.refs_4_
  86.4 2.0 collective-permute-start.6
  88.5 5.6 %collective-permute-done.4.refs_5_ = bf16[4,48,1024]{2,1,0:T(8,128)(2,1)S(1)} collective-permute-done((bf16[4,48,1024]{2,1,0:T(8,128)(2,1)S(1)}, bf16[4,48,1024]{2,1,0:T(8,128)(2,1)S(1)}, u32[]{:S(2)}, u32[]{:S(2)}) %collective-permute-start.4) | collective-permute-done | bytes 393248 | tf_op jit(solution)/shard_map/ppermute | solution.py:52
  94.1 8.4 %collective-permute-done.5.refs_6_ = bf16[4,48,1024]{2,1,0:T(8,128)(2,1)S(1)} collective-permute-done((bf16[4,48,1024]{2,1,0:T(8,128)(2,1)S(1)}, bf16[4,48,1024]{2,1,0:T(8,128)(2,1)S(1)}, u32[]{:S(2)}, u32[]{:S(2)}) %collective-permute-start.5) | collective-permute-done | bytes 393248 | tf_op jit(solution)/shard_map/ppermute | solution.py:52
  102.5 7.4 %collective-permute-done.6.refs_7_ = bf16[4,48,1024]{2,1,0:T(8,128)(2,1)S(1)} collective-permute-done((bf16[4,48,1024]{2,1,0:T(8,128)(2,1)S(1)}, bf16[4,48,1024]{2,1,0:T(8,128)(2,1)S(1)}, u32[]{:S(2)}, u32[]{:S(2)}) %collective-permute-start.6) | collective-permute-done | bytes 393248 | tf_op jit(solution)/shard_map/ppermute | solution.py:52
  109.9 1.6 copy-done.6
  116.1 15.9 %expert_forward.1 = (bf16[4,4,48,1024]{3,2,1,0:T(8,128)(2,1)S(1)}, bf16[4,4,48,1024]{3,2,1,0:T(8,128)(2,1)}, f32[384,1024]{1,0:T(8,128)S(1)}) custom-call(bf16[4,48,1024]{2,1,0:T(8,128)(2,1)S(1)} %copy-done.16, bf16[4,48,1024]{2,1,0:T(8,128)(2,1)S(1)} %copy-done.18, bf16[4,48,1024]{2,1,0:T(8,128)(2,1)S(1)} %copy-done.20, ...), custom_call_target="tpu_custom_call" | custom-call | flops 4831838208 | bytes 20971520 | tf_op jit(solution)/shard_map/expert_forward/pallas_call | solution.py:328
  136.2 4.3 %collective-permute-start.14 = (bf16[4,48,1024]{2,1,0:T(8,128)(2,1)S(1)}, bf16[4,48,1024]{2,1,0:T(8,128)(2,1)S(1)}, u32[]{:S(2)}, u32[]{:S(2)}) collective-permute-start(bf16[4,48,1024]{2,1,0:T(8,128)(2,1)S(1)} %get-tuple-element.30), channel_id=1, source_target_pairs={{0,64},{1,65},{2,194},{3,195},{64,128},{65,129},{66,2},{67,3},{128... | collective-permute-start | bytes 1179656 | tf_op jit(solution)/shard_map/ppermute | solution.py:52
  142.8 3.0 collective-permute-start.17
  145.7 42.1 %collective-permute-done.14.refs_1_ = bf16[4,48,1024]{2,1,0:T(8,128)(2,1)S(1)} collective-permute-done((bf16[4,48,1024]{2,1,0:T(8,128)(2,1)S(1)}, bf16[4,48,1024]{2,1,0:T(8,128)(2,1)S(1)}, u32[]{:S(2)}, u32[]{:S(2)}) %collective-permute-start.14) | collective-permute-done | bytes 393248 | tf_op jit(solution)/shard_map/ppermute | solution.py:52
  187.8 2.6 collective-permute-start.18
  190.4 2.0 collective-permute-start.20
  192.4 3.6 %collective-permute-done.17.refs_4_ = bf16[4,48,1024]{2,1,0:T(8,128)(2,1)S(1)} collective-permute-done((bf16[4,48,1024]{2,1,0:T(8,128)(2,1)S(1)}, bf16[4,48,1024]{2,1,0:T(8,128)(2,1)S(1)}, u32[]{:S(2)}, u32[]{:S(2)}) %collective-permute-start.17) | collective-permute-done | bytes 393248 | tf_op jit(solution)/shard_map/ppermute | solution.py:52
  196.0 8.4 %collective-permute-done.18.refs_5_ = bf16[4,48,1024]{2,1,0:T(8,128)(2,1)S(1)} collective-permute-done((bf16[4,48,1024]{2,1,0:T(8,128)(2,1)S(1)}, bf16[4,48,1024]{2,1,0:T(8,128)(2,1)S(1)}, u32[]{:S(2)}, u32[]{:S(2)}) %collective-permute-start.18) | collective-permute-done | bytes 393248 | tf_op jit(solution)/shard_map/ppermute | solution.py:52
  204.4 8.4 %collective-permute-done.19.refs_6_ = bf16[4,48,1024]{2,1,0:T(8,128)(2,1)S(1)} collective-permute-done((bf16[4,48,1024]{2,1,0:T(8,128)(2,1)S(1)}, bf16[4,48,1024]{2,1,0:T(8,128)(2,1)S(1)}, u32[]{:S(2)}, u32[]{:S(2)}) %collective-permute-start.19) | collective-permute-done | bytes 393248 | tf_op jit(solution)/shard_map/ppermute | solution.py:52
  212.9 6.4 %collective-permute-done.20.refs_7_ = bf16[4,48,1024]{2,1,0:T(8,128)(2,1)S(1)} collective-permute-done((bf16[4,48,1024]{2,1,0:T(8,128)(2,1)S(1)}, bf16[4,48,1024]{2,1,0:T(8,128)(2,1)S(1)}, u32[]{:S(2)}, u32[]{:S(2)}) %collective-permute-start.20) | collective-permute-done | bytes 393248 | tf_op jit(solution)/shard_map/ppermute | solution.py:52
  220.7 12.6 %expert_backward.1 = (bf16[4,4,48,1024]{3,2,1,0:T(8,128)(2,1)S(1)}, bf16[4,4,48,1024]{3,2,1,0:T(8,128)(2,1)}) custom-call(bf16[4,48,1024]{2,1,0:T(8,128)(2,1)S(1)} %get-tuple-element.29.refs_0_, bf16[4,48,1024]{2,1,0:T(8,128)(2,1)S(1)} %collective-permute-done.14.refs_1_, bf16[4,48,1024]{2,1,0:T(8,128)(2,1)S(1)} %collective-permute-done.15.refs_2_, ...), custom_call_target="tpu_custom_call" | custom-call | flops 4831838208 | bytes 20971520 | tf_op jit(solution)/shard_map/expert_backward/pallas_call | solution.py:328
  234.2 2.1 add_convert_fusion.1
  237.9 3.0 collective-permute-start.12
  242.1 12.2 %collective-permute-done.11.b1 = bf16[4,48,1024]{2,1,0:T(8,128)(2,1)S(1)} collective-permute-done((bf16[4,48,1024]{2,1,0:T(8,128)(2,1)S(1)}, bf16[4,48,1024]{2,1,0:T(8,128)(2,1)S(1)}, u32[]{:S(2)}, u32[]{:S(2)}) %collective-permute-start.11) | collective-permute-done | bytes 393248 | tf_op jit(solution)/shard_map/ppermute | solution.py:52
  254.4 12.7 %collective-permute-done.12.b2 = bf16[4,48,1024]{2,1,0:T(8,128)(2,1)S(1)} collective-permute-done((bf16[4,48,1024]{2,1,0:T(8,128)(2,1)S(1)}, bf16[4,48,1024]{2,1,0:T(8,128)(2,1)S(1)}, u32[]{:S(2)}, u32[]{:S(2)}) %collective-permute-start.12) | collective-permute-done | bytes 393248 | tf_op jit(solution)/shard_map/ppermute | solution.py:52
  267.0 4.5 %collective-permute-done.13.b3 = bf16[4,48,1024]{2,1,0:T(8,128)(2,1)S(1)} collective-permute-done((bf16[4,48,1024]{2,1,0:T(8,128)(2,1)S(1)}, bf16[4,48,1024]{2,1,0:T(8,128)(2,1)S(1)}, u32[]{:S(2)}, u32[]{:S(2)}) %collective-permute-start.13) | collective-permute-done | bytes 393248 | tf_op jit(solution)/shard_map/ppermute | solution.py:52
  271.6 3.0 unshuffle.2
  274.6 5.0 %all-to-all-start.1 = ((bf16[16,48,1024]{2,1,0:T(8,128)(2,1)}), bf16[16,48,1024]{2,1,0:T(8,128)(2,1)S(1)}, u32[]{:S(2)}, u32[]{:S(2)}) async-start(bf16[16,48,1024]{2,1,0:T(8,128)(2,1)} %bitcast.13), calls=%async_computation.1 | async-start | bytes 3145728 | tf_op jit(solution)/shard_map/all_to_all | solution.py:56
  279.6 5.3 %collective-permute-done.21 = bf16[4,4,48,1024]{3,2,1,0:T(8,128)(2,1)} collective-permute-done((bf16[4,4,48,1024]{3,2,1,0:T(8,128)(2,1)}, bf16[4,4,48,1024]{3,2,1,0:T(8,128)(2,1)}, u32[]{:S(2)}, u32[]{:S(2)}) %collective-permute-start.21) | collective-permute-done | bytes 1572896 | tf_op jit(solution)/shard_map/ppermute | solution.py:52
  284.9 2.1 add_convert_fusion
  288.1 3.5 collective-permute-start.23
  292.9 13.4 %collective-permute-done.22.b1 = bf16[4,48,1024]{2,1,0:T(8,128)(2,1)S(1)} collective-permute-done((bf16[4,48,1024]{2,1,0:T(8,128)(2,1)S(1)}, bf16[4,48,1024]{2,1,0:T(8,128)(2,1)S(1)}, u32[]{:S(2)}, u32[]{:S(2)}) %collective-permute-start.22) | collective-permute-done | bytes 393248 | tf_op jit(solution)/shard_map/ppermute | solution.py:52
  306.3 11.8 %collective-permute-done.23.b2 = bf16[4,48,1024]{2,1,0:T(8,128)(2,1)S(1)} collective-permute-done((bf16[4,48,1024]{2,1,0:T(8,128)(2,1)S(1)}, bf16[4,48,1024]{2,1,0:T(8,128)(2,1)S(1)}, u32[]{:S(2)}, u32[]{:S(2)}) %collective-permute-start.23) | collective-permute-done | bytes 393248 | tf_op jit(solution)/shard_map/ppermute | solution.py:52
  318.1 4.1 %collective-permute-done.24.b3 = bf16[4,48,1024]{2,1,0:T(8,128)(2,1)S(1)} collective-permute-done((bf16[4,48,1024]{2,1,0:T(8,128)(2,1)S(1)}, bf16[4,48,1024]{2,1,0:T(8,128)(2,1)S(1)}, u32[]{:S(2)}, u32[]{:S(2)}) %collective-permute-start.24) | collective-permute-done | bytes 393248 | tf_op jit(solution)/shard_map/ppermute | solution.py:52
  322.2 3.1 unshuffle.3
  325.3 5.0 %all-to-all-start.3 = ((bf16[16,48,1024]{2,1,0:T(8,128)(2,1)}), bf16[16,48,1024]{2,1,0:T(8,128)(2,1)S(1)}, u32[]{:S(2)}, u32[]{:S(2)}) async-start(bf16[16,48,1024]{2,1,0:T(8,128)(2,1)} %bitcast.21), calls=%async_computation.3 | async-start | bytes 3145728 | tf_op jit(solution)/shard_map/all_to_all | solution.py:56
  332.4 11.3 %attention.1 = (bf16[128,2048]{1,0:T(8,128)(2,1)}, bf16[128,2048]{1,0:T(8,128)(2,1)}, bf16[128,128]{1,0:T(8,128)(2,1)}, bf16[128,128]{1,0:T(8,128)(2,1)}) custom-call(bf16[128,2048]{1,0:T(8,128)(2,1)S(1)} %copy-done.12, bf16[128,128]{1,0:T(8,128)(2,1)S(1)} %copy-done.23, bf16[128,128]{1,0:T(8,128)(2,1)S(1)} %copy-done.24, bf16[128,2048]{1,0:T(8,128)(2,1)S(1)} %copy-done.13), custom_call_target="tpu_custom_call" | custom-call | flops 469762048 | bytes 10485760 | tf_op jit(solution)/shard_map/attention/pallas_call | solution.py:395
  343.8 3.8 %combine.2 = bf16[128,4096]{1,0:T(8,128)(2,1)} custom-call(s32[2]{0:T(128)S(1)} %pad_add_fusion.where, s32[1,128]{1,0:T(1,128)S(1)} %bitcast.39, s32[128,1]{1,0:T(8,128)S(1)} %copy.22.ids_col, s32[128,1]{1,0:T(8,128)S(1)} %copy.23.level_col, bf16[768,1024]{1,0:T(8,128)(2,1)S(1)} %bitcast.32), custom_call_target="tpu_custom_call" | custom-call | flops 805306368 | bytes 3145728 | tf_op jit(solution)/shard_map/combine/pallas_call | solution.py:140
  347.5 3.7 %all-to-all-done.3 = bf16[16,48,1024]{2,1,0:T(8,128)(2,1)S(1)} async-done(((bf16[16,48,1024]{2,1,0:T(8,128)(2,1)}), bf16[16,48,1024]{2,1,0:T(8,128)(2,1)S(1)}, u32[]{:S(2)}, u32[]{:S(2)}) %all-to-all-start.3) | async-done | bytes 1572896 | tf_op jit(solution)/shard_map/all_to_all | solution.py:56
  351.3 3.7 %combine.3 = bf16[128,4096]{1,0:T(8,128)(2,1)} custom-call(s32[2]{0:T(128)S(1)} %pad_add_fusion.where, s32[1,128]{1,0:T(1,128)S(1)} %bitcast.40, s32[128,1]{1,0:T(8,128)S(1)} %copy.22.ids_col, s32[128,1]{1,0:T(8,128)S(1)} %copy.23.level_col, bf16[768,1024]{1,0:T(8,128)(2,1)S(1)} %bitcast.34), custom_call_target="tpu_custom_call" | custom-call | flops 805306368 | bytes 3145728 | tf_op jit(solution)/shard_map/combine/pallas_call | solution.py:140
  (90 shorter events, 28.8 us)
Async XLA Ops:
  2.8 1.2 copy-start.10
  7.7 31.6 %copy-start.27 = (bf16[768,768]{1,0:T(8,128)(2,1)S(1)}, bf16[768,768]{1,0:T(8,128)(2,1)}, u32[]{:S(2)}) copy-start(bf16[768,768]{1,0:T(8,128)(2,1)} %constant.38.clone.matrix) | copy-start | bytes 3538948
  7.7 31.6 %all-to-all-start = ((bf16[16,48,1024]{2,1,0:T(8,128)(2,1)}), bf16[16,48,1024]{2,1,0:T(8,128)(2,1)S(1)}, u32[]{:S(2)}, u32[]{:S(2)}) async-start(bf16[16,48,1024]{2,1,0:T(8,128)(2,1)} %bitcast.4), calls=%async_computation | async-start | bytes 3145728 | tf_op jit(solution)/shard_map/all_to_all | solution.py:56
  14.9 71.6 %collective-permute-start.7 = (bf16[4096,256]{1,0:T(8,128)(2,1)}, bf16[4096,256]{1,0:T(8,128)(2,1)}, u32[]{:S(2)}, u32[]{:S(2)}) collective-permute-start(bf16[4096,256]{1,0:T(8,128)(2,1)} %bitcast.41), channel_id=1, source_target_pairs={{0,1},{1,0},{2,3},{3,2},{64,65},{65,64},{66,67},{67,66},{128,129},... | collective-permute-start | bytes 6291464 | tf_op jit(solution)/shard_map/ppermute | solution.py:52
  15.0 73.5 %collective-permute-start.8 = (bf16[4096,256]{1,0:T(8,128)(2,1)}, bf16[4096,256]{1,0:T(8,128)(2,1)}, u32[]{:S(2)}, u32[]{:S(2)}) collective-permute-start(bf16[4096,256]{1,0:T(8,128)(2,1)} %bitcast.44), channel_id=1, source_target_pairs={{0,1},{1,0},{2,3},{3,2},{64,65},{65,64},{66,67},{67,66},{128,129},... | collective-permute-start | bytes 6291464 | tf_op jit(solution)/shard_map/ppermute | solution.py:52
  15.5 73.0 %collective-permute-start.9 = (bf16[256,4096]{1,0:T(8,128)(2,1)}, bf16[256,4096]{1,0:T(8,128)(2,1)}, u32[]{:S(2)}, u32[]{:S(2)}) collective-permute-start(bf16[256,4096]{1,0:T(8,128)(2,1)} %bitcast.47), channel_id=1, source_target_pairs={{0,1},{1,0},{2,3},{3,2},{64,65},{65,64},{66,67},{67,66},{128,129},... | collective-permute-start | bytes 6291464 | tf_op jit(solution)/shard_map/ppermute | solution.py:52
  39.3 10.7 %copy-start.3 = (s32[128,1]{0,1:T(1,128)S(1)}, s32[128,1]{0,1:T(1,128)}, u32[]{:S(2)}) copy-start(s32[128,1]{0,1:T(1,128)} %param.18) | copy-start | bytes 1540
  39.3 10.7 %copy-start.5 = (s32[128,1]{0,1:T(1,128)S(1)}, s32[128,1]{0,1:T(1,128)}, u32[]{:S(2)}) copy-start(s32[128,1]{0,1:T(1,128)} %param.17) | copy-start | bytes 1540
  39.3 10.7 %copy-start.11 = (bf16[128,4096]{1,0:T(8,128)(2,1)S(1)}, bf16[128,4096]{1,0:T(8,128)(2,1)}, u32[]{:S(2)}) copy-start(bf16[128,4096]{1,0:T(8,128)(2,1)} %x_ref.3) | copy-start | bytes 3145732
  42.7 20.7 %collective-permute-start = (bf16[4,48,1024]{2,1,0:T(8,128)(2,1)}, bf16[4,48,1024]{2,1,0:T(8,128)(2,1)S(1)}, u32[]{:S(2)}, u32[]{:S(2)}) collective-permute-start(bf16[4,48,1024]{2,1,0:T(8,128)(2,1)} %get-tuple-element.24), channel_id=1, source_target_pairs={{0,64},{1,65},{2,194},{3,195},{64,128},{65,129},{66,2},{67,3},{128... | collective-permute-start | bytes 1179656 | tf_op jit(solution)/shard_map/ppermute | solution.py:52
  48.1 25.6 %collective-permute-start.1 = (bf16[4,48,1024]{2,1,0:T(8,128)(2,1)}, bf16[4,48,1024]{2,1,0:T(8,128)(2,1)S(1)}, u32[]{:S(2)}, u32[]{:S(2)}) collective-permute-start(bf16[4,48,1024]{2,1,0:T(8,128)(2,1)} %get-tuple-element.25), channel_id=1, source_target_pairs={{0,130},{1,131},{2,128},{3,129},{64,194},{65,195},{66,192},{67,193... | collective-permute-start | bytes 1179656 | tf_op jit(solution)/shard_map/ppermute | solution.py:52
  53.6 9.8 %copy-start.22 = (bf16[4,48,1024]{2,1,0:T(8,128)(2,1)S(1)}, bf16[4,48,1024]{2,1,0:T(8,128)(2,1)}, u32[]{:S(2)}) copy-start(bf16[4,48,1024]{2,1,0:T(8,128)(2,1)} %copy-done.21) | copy-start | bytes 1179652
  53.6 20.1 %copy-start.15 = (bf16[4,48,1024]{2,1,0:T(8,128)(2,1)S(1)}, bf16[4,48,1024]{2,1,0:T(8,128)(2,1)}, u32[]{:S(2)}) copy-start(bf16[4,48,1024]{2,1,0:T(8,128)(2,1)} %copy-done.14) | copy-start | bytes 1179652
  53.6 79.9 %all-to-all-start.2 = ((bf16[16,48,1024]{2,1,0:T(8,128)(2,1)}), bf16[16,48,1024]{2,1,0:T(8,128)(2,1)S(1)}, u32[]{:S(2)}, u32[]{:S(2)}) async-start(bf16[16,48,1024]{2,1,0:T(8,128)(2,1)} %bitcast.15), calls=%async_computation.2 | async-start | bytes 3145728 | tf_op jit(solution)/shard_map/all_to_all | solution.py:56
  63.4 15.4 %collective-permute-start.2 = (bf16[4,48,1024]{2,1,0:T(8,128)(2,1)S(1)}, bf16[4,48,1024]{2,1,0:T(8,128)(2,1)S(1)}, u32[]{:S(2)}, u32[]{:S(2)}) collective-permute-start(bf16[4,48,1024]{2,1,0:T(8,128)(2,1)S(1)} %copy-done.22), channel_id=1, source_target_pairs={{0,194},{1,195},{2,64},{3,65},{64,2},{65,3},{66,128},{67,129},{128... | collective-permute-start | bytes 1179656 | tf_op jit(solution)/shard_map/ppermute | solution.py:52
  73.7 12.0 %collective-permute-start.3 = (bf16[4,48,1024]{2,1,0:T(8,128)(2,1)S(1)}, bf16[4,48,1024]{2,1,0:T(8,128)(2,1)S(1)}, u32[]{:S(2)}, u32[]{:S(2)}) collective-permute-start(bf16[4,48,1024]{2,1,0:T(8,128)(2,1)S(1)} %copy-done.15), channel_id=1, source_target_pairs={{0,2},{1,3},{2,0},{3,1},{64,66},{65,67},{66,64},{67,65},{128,130},... | collective-permute-start | bytes 1179656 | tf_op jit(solution)/shard_map/ppermute | solution.py:52
  78.8 15.3 %collective-permute-start.4 = (bf16[4,48,1024]{2,1,0:T(8,128)(2,1)S(1)}, bf16[4,48,1024]{2,1,0:T(8,128)(2,1)S(1)}, u32[]{:S(2)}, u32[]{:S(2)}) collective-permute-start(bf16[4,48,1024]{2,1,0:T(8,128)(2,1)S(1)} %collective-permute-done.refs_1_), channel_id=1, source_target_pairs={{0,2},{1,3},{2,0},{3,1},{64,66},{65,67},{66,64},{67,65},{128,130},... | collective-permute-start | bytes 1179656 | tf_op jit(solution)/shard_map/ppermute | solution.py:52
  85.7 16.9 %collective-permute-start.5 = (bf16[4,48,1024]{2,1,0:T(8,128)(2,1)S(1)}, bf16[4,48,1024]{2,1,0:T(8,128)(2,1)S(1)}, u32[]{:S(2)}, u32[]{:S(2)}) collective-permute-start(bf16[4,48,1024]{2,1,0:T(8,128)(2,1)S(1)} %collective-permute-done.1.refs_2_), channel_id=1, source_target_pairs={{0,2},{1,3},{2,0},{3,1},{64,66},{65,67},{66,64},{67,65},{128,130},... | collective-permute-start | bytes 1179656 | tf_op jit(solution)/shard_map/ppermute | solution.py:52
  86.4 23.5 %collective-permute-start.6 = (bf16[4,48,1024]{2,1,0:T(8,128)(2,1)S(1)}, bf16[4,48,1024]{2,1,0:T(8,128)(2,1)S(1)}, u32[]{:S(2)}, u32[]{:S(2)}) collective-permute-start(bf16[4,48,1024]{2,1,0:T(8,128)(2,1)S(1)} %collective-permute-done.2.refs_3_), channel_id=1, source_target_pairs={{0,2},{1,3},{2,0},{3,1},{64,66},{65,67},{66,64},{67,65},{128,130},... | collective-permute-start | bytes 1179656 | tf_op jit(solution)/shard_map/ppermute | solution.py:52
  109.9 1.6 copy-start.6
  111.5 1.6 copy-start.8
  133.2 101.0 %collective-permute-start.10 = (bf16[4,4,48,1024]{3,2,1,0:T(8,128)(2,1)}, bf16[4,4,48,1024]{3,2,1,0:T(8,128)(2,1)}, u32[]{:S(2)}, u32[]{:S(2)}) collective-permute-start(bf16[4,4,48,1024]{3,2,1,0:T(8,128)(2,1)} %get-tuple-element.28), channel_id=1, source_target_pairs={{0,2},{1,3},{2,0},{3,1},{64,66},{65,67},{66,64},{67,65},{128,130},... | collective-permute-start | bytes 4718600 | tf_op jit(solution)/shard_map/ppermute | solution.py:52
  133.5 1.3 copy-start.28
  134.8 84.6 %copy-start.7 = (bf16[1,4096,256]{2,1,0:T(8,128)(2,1)S(1)}, bf16[1,4096,256]{2,1,0:T(8,128)(2,1)}, u32[]{:S(2)}) copy-start(bf16[1,4096,256]{2,1,0:T(8,128)(2,1)} %param.19) | copy-start | bytes 6291460
  134.8 84.6 %copy-start.9 = (bf16[1,4096,256]{2,1,0:T(8,128)(2,1)S(1)}, bf16[1,4096,256]{2,1,0:T(8,128)(2,1)}, u32[]{:S(2)}) copy-start(bf16[1,4096,256]{2,1,0:T(8,128)(2,1)} %param.20) | copy-start | bytes 6291460
  136.2 51.6 %collective-permute-start.14 = (bf16[4,48,1024]{2,1,0:T(8,128)(2,1)S(1)}, bf16[4,48,1024]{2,1,0:T(8,128)(2,1)S(1)}, u32[]{:S(2)}, u32[]{:S(2)}) collective-permute-start(bf16[4,48,1024]{2,1,0:T(8,128)(2,1)S(1)} %get-tuple-element.30), channel_id=1, source_target_pairs={{0,64},{1,65},{2,194},{3,195},{64,128},{65,129},{66,2},{67,3},{128... | collective-permute-start | bytes 1179656 | tf_op jit(solution)/shard_map/ppermute | solution.py:52
  140.5 49.9 %collective-permute-start.15 = (bf16[4,48,1024]{2,1,0:T(8,128)(2,1)S(1)}, bf16[4,48,1024]{2,1,0:T(8,128)(2,1)S(1)}, u32[]{:S(2)}, u32[]{:S(2)}) collective-permute-start(bf16[4,48,1024]{2,1,0:T(8,128)(2,1)S(1)} %get-tuple-element.31), channel_id=1, source_target_pairs={{0,130},{1,131},{2,128},{3,129},{64,194},{65,195},{66,192},{67,193... | collective-permute-start | bytes 1179656 | tf_op jit(solution)/shard_map/ppermute | solution.py:52
  141.7 48.7 %collective-permute-start.16 = (bf16[4,48,1024]{2,1,0:T(8,128)(2,1)S(1)}, bf16[4,48,1024]{2,1,0:T(8,128)(2,1)S(1)}, u32[]{:S(2)}, u32[]{:S(2)}) collective-permute-start(bf16[4,48,1024]{2,1,0:T(8,128)(2,1)S(1)} %get-tuple-element.32), channel_id=1, source_target_pairs={{0,194},{1,195},{2,64},{3,65},{64,2},{65,3},{66,128},{67,129},{128... | collective-permute-start | bytes 1179656 | tf_op jit(solution)/shard_map/ppermute | solution.py:52
  142.8 53.3 %collective-permute-start.17 = (bf16[4,48,1024]{2,1,0:T(8,128)(2,1)S(1)}, bf16[4,48,1024]{2,1,0:T(8,128)(2,1)S(1)}, u32[]{:S(2)}, u32[]{:S(2)}) collective-permute-start(bf16[4,48,1024]{2,1,0:T(8,128)(2,1)S(1)} %get-tuple-element.29.refs_0_), channel_id=1, source_target_pairs={{0,2},{1,3},{2,0},{3,1},{64,66},{65,67},{66,64},{67,65},{128,130},... | collective-permute-start | bytes 1179656 | tf_op jit(solution)/shard_map/ppermute | solution.py:52
  187.8 16.7 %collective-permute-start.18 = (bf16[4,48,1024]{2,1,0:T(8,128)(2,1)S(1)}, bf16[4,48,1024]{2,1,0:T(8,128)(2,1)S(1)}, u32[]{:S(2)}, u32[]{:S(2)}) collective-permute-start(bf16[4,48,1024]{2,1,0:T(8,128)(2,1)S(1)} %collective-permute-done.14.refs_1_), channel_id=1, source_target_pairs={{0,2},{1,3},{2,0},{3,1},{64,66},{65,67},{66,64},{67,65},{128,130},... | collective-permute-start | bytes 1179656 | tf_op jit(solution)/shard_map/ppermute | solution.py:52
  190.4 22.5 %collective-permute-start.19 = (bf16[4,48,1024]{2,1,0:T(8,128)(2,1)S(1)}, bf16[4,48,1024]{2,1,0:T(8,128)(2,1)S(1)}, u32[]{:S(2)}, u32[]{:S(2)}) collective-permute-start(bf16[4,48,1024]{2,1,0:T(8,128)(2,1)S(1)} %collective-permute-done.15.refs_2_), channel_id=1, source_target_pairs={{0,2},{1,3},{2,0},{3,1},{64,66},{65,67},{66,64},{67,65},{128,130},... | collective-permute-start | bytes 1179656 | tf_op jit(solution)/shard_map/ppermute | solution.py:52
  190.4 28.9 %collective-permute-start.20 = (bf16[4,48,1024]{2,1,0:T(8,128)(2,1)S(1)}, bf16[4,48,1024]{2,1,0:T(8,128)(2,1)S(1)}, u32[]{:S(2)}, u32[]{:S(2)}) collective-permute-start(bf16[4,48,1024]{2,1,0:T(8,128)(2,1)S(1)} %collective-permute-done.16.refs_3_), channel_id=1, source_target_pairs={{0,2},{1,3},{2,0},{3,1},{64,66},{65,67},{66,64},{67,65},{128,130},... | collective-permute-start | bytes 1179656 | tf_op jit(solution)/shard_map/ppermute | solution.py:52
  219.3 1.4 copy-start.30
  233.3 3.0 copy-start
  233.3 51.6 %collective-permute-start.21 = (bf16[4,4,48,1024]{3,2,1,0:T(8,128)(2,1)}, bf16[4,4,48,1024]{3,2,1,0:T(8,128)(2,1)}, u32[]{:S(2)}, u32[]{:S(2)}) collective-permute-start(bf16[4,4,48,1024]{3,2,1,0:T(8,128)(2,1)} %get-tuple-element.35), channel_id=1, source_target_pairs={{0,2},{1,3},{2,0},{3,1},{64,66},{65,67},{66,64},{67,65},{128,130},... | collective-permute-start | bytes 4718600 | tf_op jit(solution)/shard_map/ppermute | solution.py:52
  236.3 35.3 %copy-start.25 = (bf16[768,768]{1,0:T(8,128)(2,1)S(1)}, bf16[768,768]{1,0:T(8,128)(2,1)}, u32[]{:S(2)}) copy-start(bf16[768,768]{1,0:T(8,128)(2,1)} %constant.39.clone.matrix) | copy-start | bytes 3538948
  236.4 17.9 %collective-permute-start.11 = (bf16[4,48,1024]{2,1,0:T(8,128)(2,1)S(1)}, bf16[4,48,1024]{2,1,0:T(8,128)(2,1)S(1)}, u32[]{:S(2)}, u32[]{:S(2)}) collective-permute-start(bf16[4,48,1024]{2,1,0:T(8,128)(2,1)S(1)} %get-tuple-element.46), channel_id=1, source_target_pairs={{64,0},{65,1},{194,2},{195,3},{128,64},{129,65},{2,66},{3,67},{192... | collective-permute-start | bytes 1179656 | tf_op jit(solution)/shard_map/ppermute | solution.py:52
  237.9 29.1 %collective-permute-start.12 = (bf16[4,48,1024]{2,1,0:T(8,128)(2,1)S(1)}, bf16[4,48,1024]{2,1,0:T(8,128)(2,1)S(1)}, u32[]{:S(2)}, u32[]{:S(2)}) collective-permute-start(bf16[4,48,1024]{2,1,0:T(8,128)(2,1)S(1)} %get-tuple-element.45), channel_id=1, source_target_pairs={{130,0},{131,1},{128,2},{129,3},{194,64},{195,65},{192,66},{193,67... | collective-permute-start | bytes 1179656 | tf_op jit(solution)/shard_map/ppermute | solution.py:52
  240.8 30.7 %collective-permute-start.13 = (bf16[4,48,1024]{2,1,0:T(8,128)(2,1)S(1)}, bf16[4,48,1024]{2,1,0:T(8,128)(2,1)S(1)}, u32[]{:S(2)}, u32[]{:S(2)}) collective-permute-start(bf16[4,48,1024]{2,1,0:T(8,128)(2,1)S(1)} %get-tuple-element.44), channel_id=1, source_target_pairs={{194,0},{195,1},{64,2},{65,3},{2,64},{3,65},{128,66},{129,67},{66,... | collective-permute-start | bytes 1179656 | tf_op jit(solution)/shard_map/ppermute | solution.py:52
  274.6 10.3 %copy-start.1 = (bf16[4,4,48,1024]{3,2,1,0:T(8,128)(2,1)S(1)}, bf16[4,4,48,1024]{3,2,1,0:T(8,128)(2,1)}, u32[]{:S(2)}) copy-start(bf16[4,4,48,1024]{3,2,1,0:T(8,128)(2,1)} %copy-done) | copy-start | bytes 4718596
  274.6 50.7 %all-to-all-start.1 = ((bf16[16,48,1024]{2,1,0:T(8,128)(2,1)}), bf16[16,48,1024]{2,1,0:T(8,128)(2,1)S(1)}, u32[]{:S(2)}, u32[]{:S(2)}) async-start(bf16[16,48,1024]{2,1,0:T(8,128)(2,1)} %bitcast.13), calls=%async_computation.1 | async-start | bytes 3145728 | tf_op jit(solution)/shard_map/all_to_all | solution.py:56
  287.0 35.2 %copy-start.26 = (bf16[768,768]{1,0:T(8,128)(2,1)S(1)}, bf16[768,768]{1,0:T(8,128)(2,1)}, u32[]{:S(2)}) copy-start(bf16[768,768]{1,0:T(8,128)(2,1)} %constant.39.clone.matrix) | copy-start | bytes 3538948
  287.2 19.1 %collective-permute-start.22 = (bf16[4,48,1024]{2,1,0:T(8,128)(2,1)S(1)}, bf16[4,48,1024]{2,1,0:T(8,128)(2,1)S(1)}, u32[]{:S(2)}, u32[]{:S(2)}) collective-permute-start(bf16[4,48,1024]{2,1,0:T(8,128)(2,1)S(1)} %get-tuple-element.42), channel_id=1, source_target_pairs={{64,0},{65,1},{194,2},{195,3},{128,64},{129,65},{2,66},{3,67},{192... | collective-permute-start | bytes 1179656 | tf_op jit(solution)/shard_map/ppermute | solution.py:52
  288.1 30.0 %collective-permute-start.23 = (bf16[4,48,1024]{2,1,0:T(8,128)(2,1)S(1)}, bf16[4,48,1024]{2,1,0:T(8,128)(2,1)S(1)}, u32[]{:S(2)}, u32[]{:S(2)}) collective-permute-start(bf16[4,48,1024]{2,1,0:T(8,128)(2,1)S(1)} %get-tuple-element.41), channel_id=1, source_target_pairs={{130,0},{131,1},{128,2},{129,3},{194,64},{195,65},{192,66},{193,67... | collective-permute-start | bytes 1179656 | tf_op jit(solution)/shard_map/ppermute | solution.py:52
  291.6 30.6 %collective-permute-start.24 = (bf16[4,48,1024]{2,1,0:T(8,128)(2,1)S(1)}, bf16[4,48,1024]{2,1,0:T(8,128)(2,1)S(1)}, u32[]{:S(2)}, u32[]{:S(2)}) collective-permute-start(bf16[4,48,1024]{2,1,0:T(8,128)(2,1)S(1)} %get-tuple-element.40), channel_id=1, source_target_pairs={{194,0},{195,1},{64,2},{65,3},{2,64},{3,65},{128,66},{129,67},{66,... | collective-permute-start | bytes 1179656 | tf_op jit(solution)/shard_map/ppermute | solution.py:52
  325.3 5.1 %copy-start.23 = (bf16[128,128]{1,0:T(8,128)(2,1)S(1)}, bf16[128,128]{1,0:T(8,128)(2,1)}, u32[]{:S(2)}) copy-start(bf16[128,128]{1,0:T(8,128)(2,1)} %k_ref.1) | copy-start | bytes 98308
  325.3 5.1 %copy-start.24 = (bf16[128,128]{1,0:T(8,128)(2,1)S(1)}, bf16[128,128]{1,0:T(8,128)(2,1)}, u32[]{:S(2)}) copy-start(bf16[128,128]{1,0:T(8,128)(2,1)} %v_ref.1) | copy-start | bytes 98308
  325.3 26.0 %all-to-all-start.3 = ((bf16[16,48,1024]{2,1,0:T(8,128)(2,1)}), bf16[16,48,1024]{2,1,0:T(8,128)(2,1)S(1)}, u32[]{:S(2)}, u32[]{:S(2)}) async-start(bf16[16,48,1024]{2,1,0:T(8,128)(2,1)} %bitcast.21), calls=%async_computation.3 | async-start | bytes 3145728 | tf_op jit(solution)/shard_map/all_to_all | solution.py:56
  (12 other events, 10.6 us)

commit v2 on v1

v2 whole, which is shorter than its diff:
```python
import functools

import jax
import jax.numpy as jnp
from jax import lax
from jax.experimental import pallas as pl
from jax.experimental.pallas import tpu as pltpu
from jax.sharding import PartitionSpec as P

HD = 128
AXES = ("dp", "tensor")
SLOTS = 3
QUARTERS = 4
BLK = 48
VMEM_LIMIT = 40 * 1024 * 1024
BF = jnp.bfloat16
F32 = jnp.float32
NT = (((1,), (1,)), ((), ()))
TN = (((0,), (0,)), ((), ()))


def linear(x, y, z, core):
    return ((z // 2) * 16 + y * 4 + x) * 4 + (z % 2) * 2 + core


def moves(target):
    pairs = []
    for x in range(4):
        for y in range(4):
            for z in range(8):
                for core in range(2):
                    z_to, core_to = target(z, core)
                    pairs.append((linear(x, y, z, core), linear(x, y, z_to % 8, core_to)))
    return pairs


INNER = moves(lambda z, c: (z ^ 1, c))
CORES = moves(lambda z, c: (z, 1 - c))
NEAR = [
    moves(lambda z, c: (z - 2 if z % 2 else z + 2, c)),
    moves(lambda z, c: (z + 3 if z % 2 else z - 3, c)),
    moves(lambda z, c: (z + 1 if z % 2 else z - 1, c)),
]
BACK = [[(b, a) for a, b in perm] for perm in NEAR]
PLANES = [
    [linear(x, y, z, c) for y in range(4) for x in range(4)] for z in range(8) for c in range(2)
]


def send(value, perm):
    return lax.ppermute(value, AXES, perm)


def plane_exchange(value):
    return lax.all_to_all(value, AXES, 0, 0, axis_index_groups=PLANES, tiled=True)


def params(**more):
    return pltpu.CompilerParams(vmem_limit_bytes=VMEM_LIMIT, **more)


WHOLE = pl.BlockSpec(memory_space=pltpu.VMEM)


def cost(flops, nbytes):
    return pl.CostEstimate(flops=flops, bytes_accessed=nbytes, transcendentals=0)


def first_row(ids, rank, where):
    pair, odd = where[0], where[1]
    turn = ((ids >> 4) - pair) & 3
    turn = jnp.where(odd == 1, (4 - turn) & 3, turn)
    return (ids & 15) * BLK + turn * SLOTS + rank


def dispatch_kernel(where, ids_row, ids_col, level_row, x_ref, out_ref, hot, quarters, *, scaled):
    tokens = ids_row.shape[1]
    ids = ids_row[...]
    earlier = lax.broadcasted_iota(jnp.int32, (tokens, tokens), 0) < lax.broadcasted_iota(
        jnp.int32, (tokens, tokens), 1
    )
    same = jnp.where(earlier & (ids_col[...] == ids), 1, 0)
    rank = jnp.sum(same, axis=0, keepdims=True)
    base = first_row(ids, rank, where)
    rows, width = out_ref.shape
    row = lax.broadcasted_iota(jnp.int32, (rows, tokens), 0)
    if scaled:
        value = jnp.broadcast_to(level_row[...].astype(F32) * 0.125, (rows, tokens))
    else:
        value = jnp.full((rows, tokens), 1.0, F32)
    for q in range(QUARTERS):
        part = slice(q * tokens, (q + 1) * tokens)
        hot[:, part] = jnp.where(row == base + q * (4 * SLOTS), value, 0.0).astype(BF)
        quarters[part, :] = x_ref[:, q * width : (q + 1) * width]
    out_ref[...] = jnp.dot(hot[...], quarters[...], preferred_element_type=F32).astype(BF)


def dispatch(where, ids_row, ids_col, level_row, x, scaled):
    tokens, d = x.shape
    rows, width = 16 * BLK, d // QUARTERS
    out = pl.pallas_call(
        functools.partial(dispatch_kernel, scaled=scaled),
        out_shape=jax.ShapeDtypeStruct((rows, width), BF),
        in_specs=[pl.BlockSpec(memory_space=pltpu.SMEM)] + [WHOLE] * 4,
        out_specs=WHOLE,
        scratch_shapes=[
            pltpu.VMEM((rows, QUARTERS * tokens), BF),
            pltpu.VMEM((QUARTERS * tokens, width), BF),
        ],
        compiler_params=params(),
        cost_estimate=cost(2 * rows * tokens * d, 4 * rows * width),
        name="dispatch",
    )(where, ids_row, ids_col, level_row, x)
    return out.reshape(16, BLK, width)


def combine_kernel(where, ids_row, ids_col, level_col, back_ref, out_ref, *, scaled):
    tokens = ids_row.shape[1]
    ids = ids_col[...]
    earlier = lax.broadcasted_iota(jnp.int32, (tokens, tokens), 1) < lax.broadcasted_iota(
        jnp.int32, (tokens, tokens), 0
    )
    same = jnp.where(earlier & (ids == ids_row[...]), 1, 0)
    rank = jnp.sum(same, axis=1, keepdims=True)
    base = first_row(ids, rank, where)
    rows, width = back_ref.shape
    row = lax.broadcasted_iota(jnp.int32, (tokens, rows), 1)
    if scaled:
        value = jnp.broadcast_to(level_col[...].astype(F32) * 0.125, (tokens, rows))
    else:
        value = jnp.full((tokens, rows), 1.0, F32)
    for q in range(QUARTERS):
        hot = jnp.where(row == base + q * (4 * SLOTS), value, 0.0).astype(BF)
        part = jnp.dot(hot, back_ref[...], preferred_element_type=F32)
        out_ref[:, q * width : (q + 1) * width] = part.astype(BF)


def combine(where, ids_row, ids_col, level_col, back, scaled):
    back = back.reshape(-1, back.shape[-1])
    rows, width = back.shape
    tokens = ids_row.shape[1]
    return pl.pallas_call(
        functools.partial(combine_kernel, scaled=scaled),
        out_shape=jax.ShapeDtypeStruct((tokens, QUARTERS * width), BF),
        in_specs=[pl.BlockSpec(memory_space=pltpu.SMEM)] + [WHOLE] * 4,
        out_specs=WHOLE,
        compiler_params=params(),
        cost_estimate=cost(2 * rows * tokens * width * QUARTERS, 4 * rows * width),
        name="combine",
    )(where, ids_row, ids_col, level_col, back)


def divide(value, by):
    return (value * ((1 << 20) // by + 1)) >> 20


def by_source_of(row):
    turn = divide(row, 192)
    rest = row - turn * 192
    quarter = divide(rest, BLK)
    rest = rest - quarter * BLK
    source = divide(rest, SLOTS)
    return source * BLK + quarter * (4 * SLOTS) + turn * SLOTS + rest - source * SLOTS


def by_turn_of(row):
    source = divide(row, BLK)
    rest = row - source * BLK
    quarter = divide(rest, 4 * SLOTS)
    rest = rest - quarter * (4 * SLOTS)
    turn = divide(rest, SLOTS)
    return turn * 192 + quarter * BLK + source * SLOTS + rest - turn * SLOTS


def one_hot(target, rows):
    row = lax.broadcasted_iota(jnp.int32, (rows, 1), 0)
    column = lax.broadcasted_iota(jnp.int32, (rows, rows), 1)
    return jnp.where(column == target(row), 1.0, 0.0).astype(BF)


def shuffle_kernel(rows_ref, *refs):
    outs, matrix = refs[:4], refs[4]
    matrix[...] = one_hot(by_source_of, matrix.shape[0])
    for turn, out in enumerate(outs):
        part = jnp.dot(
            matrix[turn * 192 : (turn + 1) * 192, :], rows_ref[...], preferred_element_type=F32
        )
        out[...] = part.astype(BF).reshape(out.shape)


def shuffle(rows):
    width = rows.shape[-1]
    return pl.pallas_call(
        shuffle_kernel,
        out_shape=[jax.ShapeDtypeStruct((QUARTERS, BLK, width), BF)] * 4,
        in_specs=[WHOLE],
        out_specs=[WHOLE] * 4,
        scratch_shapes=[pltpu.VMEM((768, 768), BF)],
        compiler_params=params(),
        cost_estimate=cost(2 * 768 * 768 * width, 4 * 768 * width),
        name="shuffle",
    )(rows.reshape(768, width))


def unshuffle_kernel(b0, b1, b2, b3, out_ref, matrix, rows):
    matrix[...] = one_hot(by_turn_of, matrix.shape[0])
    for turn, block in enumerate((b0, b1, b2, b3)):
        rows[turn * 192 : (turn + 1) * 192, :] = block[...].reshape(192, block.shape[-1])
    out_ref[...] = jnp.dot(matrix[...], rows[...], preferred_element_type=F32).astype(BF)


def unshuffle(blocks):
    width = blocks[0].shape[-1]
    out = pl.pallas_call(
        unshuffle_kernel,
        out_shape=jax.ShapeDtypeStruct((768, width), BF),
        in_specs=[WHOLE] * 4,
        out_specs=WHOLE,
        scratch_shapes=[pltpu.VMEM((768, 768), BF), pltpu.VMEM((768, width), BF)],
        compiler_params=params(),
        cost_estimate=cost(2 * 768 * 768 * width, 4 * 768 * width),
        name="unshuffle",
    )(*blocks)
    return out.reshape(16, BLK, width)


def gather_rows(blocks, rows):
    for i, block in enumerate(blocks):
        for q in range(QUARTERS):
            width = block.shape[-1]
            rows[i * BLK : (i + 1) * BLK, q * width : (q + 1) * width] = block[q]


def hidden_kernel(*refs):
    blocks, weights, (near, far, acts, rows) = refs[:8], refs[8:12], refs[12:]
    ff = weights[0].shape[1]
    half = near.shape[0]
    gather_rows(blocks, rows)
    for i, w in enumerate(weights):
        acts[:, i * ff : (i + 1) * ff] = jnp.dot(rows[...], w[...], preferred_element_type=F32)
    gate = acts[:, : 2 * ff]
    hidden = (gate * jax.nn.sigmoid(gate) * acts[:, 2 * ff :]).astype(BF)
    near[...] = hidden[:half]
    far[...] = hidden[half:]


def hidden_call(blocks, wg, wu):
    width = blocks[0].shape[-1]
    ff = wg[0].shape[1]
    rows = 8 * BLK
    part = jax.ShapeDtypeStruct((rows // 2, 2 * ff), BF)
    return pl.pallas_call(
        hidden_kernel,
        out_shape=[part, part, jax.ShapeDtypeStruct((rows, 4 * ff), F32)],
        in_specs=[WHOLE] * 12,
        out_specs=[WHOLE] * 3,
        scratch_shapes=[pltpu.VMEM((rows, QUARTERS * width), BF)],
        compiler_params=params(),
        cost_estimate=cost(8 * rows * width * QUARTERS * ff, 16 * 1024 * 1024),
        name="hidden",
    )(*blocks, *wg, *wu)


def d_hidden_kernel(*refs):
    blocks, weights, (mine, other, rows) = refs[:4], refs[4:8], refs[8:]
    ff = weights[0].shape[0]
    gather_rows(blocks, rows)
    for i, w in enumerate(weights):
        part = lax.dot_general(rows[...], w[...], NT, preferred_element_type=F32)
        out = (mine, other)[i // 2]
        out[:, (i % 2) * ff : (i % 2 + 1) * ff] = part.astype(out.dtype)


def d_hidden_call(blocks, wd):
    width = blocks[0].shape[-1]
    ff = wd[0].shape[0]
    rows = 4 * BLK
    return pl.pallas_call(
        d_hidden_kernel,
        out_shape=[
            jax.ShapeDtypeStruct((rows, 2 * ff), F32),
            jax.ShapeDtypeStruct((rows, 2 * ff), BF),
        ],
        in_specs=[WHOLE] * 8,
        out_specs=[WHOLE] * 2,
        scratch_shapes=[pltpu.VMEM((rows, QUARTERS * width), BF)],
        compiler_params=params(),
        cost_estimate=cost(8 * rows * width * QUARTERS * ff, 12 * 1024 * 1024),
        name="d_hidden",
    )(*blocks, *wd)


def store_blocks(value, outs, q):
    for i, out in enumerate(outs):
        out[q] = value[i * BLK : (i + 1) * BLK].astype(BF)


def out_kernel(near, other, wd0, wd1, wd2, wd3, *outs):
    ff = wd0.shape[0]
    width = outs[0].shape[-1]
    for q in range(QUARTERS):
        total = None
        for i, w in enumerate((wd0, wd1, wd2, wd3)):
            hidden = (near, other)[i // 2]
            part = jnp.dot(
                hidden[:, (i % 2) * ff : (i % 2 + 1) * ff],
                w[:, q * width : (q + 1) * width],
                preferred_element_type=F32,
            )
            total = part if total is None else total + part
        store_blocks(total, outs, q)


def out_call(near, other, wd):
    ff, d = wd[0].shape
    rows = near.shape[0]
    return pl.pallas_call(
        out_kernel,
        out_shape=[jax.ShapeDtypeStruct((QUARTERS, BLK, d // QUARTERS), BF)] * 4,
        in_specs=[WHOLE] * 6,
        out_specs=[WHOLE] * 4,
        compiler_params=params(),
        cost_estimate=cost(8 * rows * d * ff, 10 * 1024 * 1024),
        name="expert_out",
    )(near, other, *wd)


def grad_kernel(acts, dh, wg0, wg1, wu0, wu1, *refs, first):
    outs, dacts = refs[:4], refs[4]
    ff = wg0.shape[1]
    width = outs[0].shape[-1]
    rows = slice(first, first + dh.shape[0])
    gate = acts[rows, : 2 * ff]
    up = acts[rows, 2 * ff :]
    sigma = jax.nn.sigmoid(gate)
    d_hidden = dh[...].astype(F32)
    d_gate = d_hidden * up * sigma * (1.0 + gate * (1.0 - sigma))
    dacts[:, : 2 * ff] = d_gate.astype(BF)
    dacts[:, 2 * ff :] = (d_hidden * (gate * sigma)).astype(BF)
    for q in range(QUARTERS):
        total = None
        for i, w in enumerate((wg0, wg1, wu0, wu1)):
            part = lax.dot_general(
                dacts[:, i * ff : (i + 1) * ff],
                w[q * width : (q + 1) * width, :],
                NT,
                preferred_element_type=F32,
            )
            total = part if total is None else total + part
        store_blocks(total, outs, q)


def grad_call(acts, dh, wg, wu, first):
    d, ff = wg[0].shape
    rows = dh.shape[0]
    return pl.pallas_call(
        functools.partial(grad_kernel, first=first),
        out_shape=[jax.ShapeDtypeStruct((QUARTERS, BLK, d // QUARTERS), BF)] * 4,
        in_specs=[WHOLE] * 6,
        out_specs=[WHOLE] * 4,
        scratch_shapes=[pltpu.VMEM((rows, 4 * ff), BF)],
        compiler_params=params(),
        cost_estimate=cost(8 * rows * d * ff, 12 * 1024 * 1024),
        name="expert_grad",
    )(acts, dh, *wg, *wu)


HEADS_STEP = 4


def attention_kernel(q_ref, k_ref, v_ref, do_ref, o_ref, dq_ref, dk_ref, dv_ref, dk_acc, dv_acc):
    step = pl.program_id(0)
    length = k_ref.shape[0]
    scale = HD ** (-0.5)
    k = k_ref[...]
    v = v_ref[...]
    causal = lax.broadcasted_iota(jnp.int32, (length, length), 0) >= lax.broadcasted_iota(
        jnp.int32, (length, length), 1
    )
    dk = None
    dv = None
    for h in range(HEADS_STEP):
        cols = slice(h * HD, (h + 1) * HD)
        q = q_ref[:, cols]
        do = do_ref[:, cols]
        scores = lax.dot_general(q, k, NT, preferred_element_type=F32) * scale
        scores = jnp.where(causal, scores, -1e30)
        raised = jnp.exp(scores - jnp.max(scores, axis=1, keepdims=True))
        probs = raised / jnp.sum(raised, axis=1, keepdims=True)
        rounded = probs.astype(BF)
        o_ref[:, cols] = jnp.dot(rounded, v, preferred_element_type=F32).astype(BF)
        d_probs = lax.dot_general(do, v, NT, preferred_element_type=F32).astype(BF).astype(F32)
        inner = jnp.sum(d_probs * probs, axis=1, keepdims=True)
        d_scores = (probs * (d_probs - inner) * scale).astype(BF)
        dq_ref[:, cols] = jnp.dot(d_scores, k, preferred_element_type=F32).astype(BF)
        dk_part = lax.dot_general(d_scores, q, TN, preferred_element_type=F32)
        dv_part = lax.dot_general(rounded, do, TN, preferred_element_type=F32)
        dk = dk_part if dk is None else dk + dk_part
        dv = dv_part if dv is None else dv + dv_part

    @pl.when(step == 0)
    def _():
        dk_acc[...] = dk
        dv_acc[...] = dv

    @pl.when(step > 0)
    def _():
        dk_acc[...] = dk_acc[...] + dk
        dv_acc[...] = dv_acc[...] + dv

    @pl.when(step == pl.num_programs(0) - 1)
    def _():
        dk_ref[...] = dk_acc[...].astype(BF)
        dv_ref[...] = dv_acc[...].astype(BF)


def attention(queries, keys, values, cotangent):
    length, wide = queries.shape
    head_spec = pl.BlockSpec((length, HEADS_STEP * HD), lambda s: (0, s))
    key_spec = pl.BlockSpec((length, HD), lambda s: (0, 0))
    heads = wide // HD
    return pl.pallas_call(
        attention_kernel,
        out_shape=[
            jax.ShapeDtypeStruct(queries.shape, BF),
            jax.ShapeDtypeStruct(queries.shape, BF),
            jax.ShapeDtypeStruct(keys.shape, BF),
            jax.ShapeDtypeStruct(values.shape, BF),
        ],
        grid=(heads // HEADS_STEP,),
        in_specs=[head_spec, key_spec, key_spec, head_spec],
        out_specs=[head_spec, head_spec, key_spec, key_spec],
        scratch_shapes=[pltpu.VMEM((length, HD), F32)] * 2,
        compiler_params=params(dimension_semantics=("arbitrary",)),
        cost_estimate=cost(14 * heads * length * length * HD, 10 * 1024 * 1024),
        name="attention",
    )(queries, keys, values, cotangent)


def to_near(blocks):
    own, *others = blocks
    return [own] + [send(block, perm) for block, perm in zip(others, NEAR)]


def to_sources(blocks):
    back = [blocks[0]] + [send(block, perm) for block, perm in zip(blocks[1:], BACK)]
    return plane_exchange(unshuffle(back))


def on_device(
    layer_input,
    out_grad,
    expert_ids,
    gate_level,
    w_gate,
    w_up,
    w_down,
    attn_queries,
    attn_keys,
    attn_values,
    attn_grad,
):
    tokens = layer_input.shape[0]
    where = jnp.stack([lax.axis_index("dp") // 16, lax.axis_index("tensor") // 2]).astype(jnp.int32)
    ids_row = expert_ids.reshape(1, tokens)
    ids_col = expert_ids.reshape(tokens, 1)
    level_row = gate_level.reshape(1, tokens)
    level_col = gate_level.reshape(tokens, 1)

    down = w_down[0]
    down_other = send(down, INNER)
    wg = (w_gate[0], send(w_gate[0], CORES))
    wu = (w_up[0], send(w_up[0], CORES))
    wd = (down, send(down, CORES), down_other, send(down_other, CORES))

    x_sent = dispatch(where, ids_row, ids_col, level_row, layer_input, False)
    g_sent = dispatch(where, ids_row, ids_col, level_row, out_grad, True)
    x_rows = plane_exchange(x_sent)
    attended = attention(attn_queries, attn_keys, attn_values, attn_grad)
    x_rows, g_sent, attended = lax.optimization_barrier((x_rows, g_sent, attended))
    g_rows = plane_exchange(g_sent)

    x_near = to_near(shuffle(x_rows))
    g_blocks = shuffle(g_rows)
    x_near[2], g_blocks = lax.optimization_barrier((x_near[2], g_blocks))
    g_near = to_near(g_blocks)
    x_far = [send(block, INNER) for block in x_near]

    hidden_near, hidden_far, acts = hidden_call(x_near + x_far, wg, wu)
    hidden_other = send(hidden_far, INNER)
    dh_near, dh_far = d_hidden_call(g_near, wd)
    dh_other = send(dh_far, INNER)

    half = dh_near.shape[0]
    far_terms = grad_call(acts, dh_other, wg, wu, half)
    arrived = [send(block, INNER) for block in far_terms]
    out_blocks = out_call(hidden_near, hidden_other, wd)
    near_terms = grad_call(acts, dh_near, wg, wu, 0)
    grad_blocks = [
        (a.astype(F32) + b.astype(F32)).astype(BF) for a, b in zip(near_terms, arrived)
    ]
    out_back = to_sources(out_blocks)
    grad_back = to_sources(grad_blocks)

    moe_out = combine(where, ids_row, ids_col, level_col, out_back, True)
    grad_x = combine(where, ids_row, ids_col, level_col, grad_back, False)
    attn_out, grad_q, grad_k, grad_v = attended
    return (moe_out, grad_x, attn_out, grad_q, grad_k, grad_v)


def solution(mesh):
    in_specs = (
        P(("dp", "tensor"), None),
        P(("dp", "tensor"), None),
        P(("dp", "tensor"), None),
        P(("dp", "tensor"), None),
        P("dp", None, "tensor"),
        P("dp", None, "tensor"),
        P("dp", "tensor", None),
        P("dp", "tensor"),
        P("dp", "tensor"),
        P("dp", "tensor"),
        P("dp", "tensor"),
    )
    out_specs = (
        P(("dp", "tensor"), None),
        P(("dp", "tensor"), None),
        P("dp", "tensor"),
        P("dp", "tensor"),
        P("dp", "tensor"),
        P("dp", "tensor"),
    )
    return jax.shard_map(
        on_device, mesh=mesh, in_specs=in_specs, out_specs=out_specs, check_vma=False
    )
```

time: 356 us -> 301 us (0.85)
  waiting for transfers between devices: 205 us -> 152 us
  starting transfers between devices: 61.7 us -> 72.7 us
  local copies, waits for them, and re-layouts: 18.9 us -> 11.7 us
  Pallas kernels: 63.8 us -> 59.4 us
    ppermute x25 -> x27, waiting for transfers between devices: 178 us -> 128 us  [send(): return lax.ppermute(value, AXES, perm)]
    ppermute x25 -> x27, starting transfers between devices: 40.7 us -> 49 us  [send(): return lax.ppermute(value, AXES, perm)]
    unnamed x64 -> x44, local copies, waits for them, and re-layouts: 18.6 us -> 11.7 us
    pallas_call x2, Pallas kernels: 7.19 us -> 3.31 us  [dispatch(): pl.pallas_call(functools.partial(dispatch_kernel, scaled=scaled), out_sha...]
    pallas_call x2 -> x5, Pallas kernels: 28.5 us -> 28.3 us  [the longest x2 10.9 us: grad_call(): pl.pallas_call(functools.partial(grad_kernel, first=first), out_shape=[ja...]
  transfers between devices with their start and end apart: 29 -> 31, of which waited for: 21 -> 17; matrix products, arithmetic and copies ran while one was open for 1% -> 1% of each run, Pallas kernels for 16% -> 19%
where the time goes in v2:
time: 301 us; the launch traced here: 298 us
  waiting for transfers between devices  152 us (50%)
  starting transfers between devices  72.7 us (24%)
  Pallas kernels  59.4 us (20%)
  local copies, waits for them, and re-layouts  11.7 us (4%)
    ppermute x27, waiting for transfers between devices, send(): return lax.ppermute(value, AXES, perm)  128 us
    ppermute x27, starting transfers between devices, send(): return lax.ppermute(value, AXES, perm)  49 us
    all_to_all x4, waiting for transfers between devices, plane_exchange(): lax.all_to_all(value, AXES, 0, 0, axis_index_groups=PLANES, tiled=True)  24.1 us
    all_to_all x4, starting transfers between devices, plane_exchange(): lax.all_to_all(value, AXES, 0, 0, axis_index_groups=PLANES, tiled=True)  23.7 us
    unnamed x44, local copies, waits for them, and re-layouts  11.7 us
    pallas_call x1, Pallas kernels, attention(): pl.pallas_call(attention_kernel, out_shape=[jax.ShapeDtypeStruct(queries....  11.3 us
    pallas_call x2, Pallas kernels, grad_call(): pl.pallas_call(functools.partial(grad_kernel, first=first), out_shape=[ja...  10.9 us
    pallas_call x2, Pallas kernels, combine(): pl.pallas_call(functools.partial(combine_kernel, scaled=scaled), out_shap...  6.35 us
  transfers between devices with their start and end apart: 31, of which 17 were waited for; matrix products, arithmetic and copies ran while one was open for 1% of the time, Pallas kernels for 19%

profile of v2, /device:TPU:32, one launch (start us, length us, event | category | flops | bytes accessed | tf_op | source)
XLA Modules:
  0.0 298.3 jit_solution(13873797646748765763)
XLA Ops:
  0.6 1.9 collective-permute-start.11
  6.0 1.7 dispatch.2
  8.8 5.6 %all-to-all-start = ((bf16[16,48,1024]{2,1,0:T(8,128)(2,1)}), bf16[16,48,1024]{2,1,0:T(8,128)(2,1)}, u32[]{:S(2)}, u32[]{:S(2)}) async-start(bf16[16,48,1024]{2,1,0:T(8,128)(2,1)} %bitcast.25), calls=%async_computation | async-start | bytes 3145728 | tf_op jit(solution)/shard_map/all_to_all | solution.py:55
  16.1 11.3 %attention.1 = (bf16[128,2048]{1,0:T(8,128)(2,1)}, bf16[128,2048]{1,0:T(8,128)(2,1)}, bf16[128,128]{1,0:T(8,128)(2,1)}, bf16[128,128]{1,0:T(8,128)(2,1)}) custom-call(bf16[128,2048]{1,0:T(8,128)(2,1)S(1)} %copy-done.14, bf16[128,128]{1,0:T(8,128)(2,1)S(1)} %copy-done.19, bf16[128,128]{1,0:T(8,128)(2,1)S(1)} %copy-done.20, bf16[128,2048]{1,0:T(8,128)(2,1)S(1)} %copy-done.15), custom_call_target="tpu_custom_call" | custom-call | flops 469762048 | bytes 10485760 | tf_op jit(solution)/shard_map/attention/pallas_call | solution.py:422
  27.5 1.7 dispatch.3
  30.3 8.5 %all-to-all-done = bf16[16,48,1024]{2,1,0:T(8,128)(2,1)} async-done(((bf16[16,48,1024]{2,1,0:T(8,128)(2,1)}), bf16[16,48,1024]{2,1,0:T(8,128)(2,1)}, u32[]{:S(2)}, u32[]{:S(2)}) %all-to-all-start) | async-done | bytes 1572896 | tf_op jit(solution)/shard_map/all_to_all | solution.py:55
  38.9 4.4 %all-to-all-start.1 = ((bf16[16,48,1024]{2,1,0:T(8,128)(2,1)}), bf16[16,48,1024]{2,1,0:T(8,128)(2,1)}, u32[]{:S(2)}, u32[]{:S(2)}) async-start(bf16[16,48,1024]{2,1,0:T(8,128)(2,1)} %bitcast.24), calls=%async_computation.1 | async-start | bytes 3145728 | tf_op jit(solution)/shard_map/all_to_all | solution.py:55
  43.3 2.9 shuffle.2
  46.2 6.0 %collective-permute-start = (bf16[4,48,1024]{2,1,0:T(8,128)(2,1)S(1)}, bf16[4,48,1024]{2,1,0:T(8,128)(2,1)S(1)}, u32[]{:S(2)}, u32[]{:S(2)}) collective-permute-start(bf16[4,48,1024]{2,1,0:T(8,128)(2,1)S(1)} %get-tuple-element.52), channel_id=1, source_target_pairs={{0,64},{1,65},{2,194},{3,195},{64,128},{65,129},{66,2},{67,3},{128... | collective-permute-start | bytes 1179656 | tf_op jit(solution)/shard_map/ppermute | solution.py:51
  52.7 6.3 %collective-permute-done.refs_1_ = bf16[4,48,1024]{2,1,0:T(8,128)(2,1)S(1)} collective-permute-done((bf16[4,48,1024]{2,1,0:T(8,128)(2,1)S(1)}, bf16[4,48,1024]{2,1,0:T(8,128)(2,1)S(1)}, u32[]{:S(2)}, u32[]{:S(2)}) %collective-permute-start) | collective-permute-done | bytes 393248 | tf_op jit(solution)/shard_map/ppermute | solution.py:51
  59.0 5.0 %collective-permute-start.1 = (bf16[4,48,1024]{2,1,0:T(8,128)(2,1)S(1)}, bf16[4,48,1024]{2,1,0:T(8,128)(2,1)S(1)}, u32[]{:S(2)}, u32[]{:S(2)}) collective-permute-start(bf16[4,48,1024]{2,1,0:T(8,128)(2,1)S(1)} %get-tuple-element.53), channel_id=1, source_target_pairs={{0,130},{1,131},{2,128},{3,129},{64,194},{65,195},{66,192},{67,193... | collective-permute-start | bytes 1179656 | tf_op jit(solution)/shard_map/ppermute | solution.py:51
  64.1 13.7 %collective-permute-done.1.refs_2_ = bf16[4,48,1024]{2,1,0:T(8,128)(2,1)S(1)} collective-permute-done((bf16[4,48,1024]{2,1,0:T(8,128)(2,1)S(1)}, bf16[4,48,1024]{2,1,0:T(8,128)(2,1)S(1)}, u32[]{:S(2)}, u32[]{:S(2)}) %collective-permute-start.1) | collective-permute-done | bytes 393248 | tf_op jit(solution)/shard_map/ppermute | solution.py:51
  79.2 9.7 %collective-permute-done.2.refs_3_ = bf16[4,48,1024]{2,1,0:T(8,128)(2,1)S(1)} collective-permute-done((bf16[4,48,1024]{2,1,0:T(8,128)(2,1)S(1)}, bf16[4,48,1024]{2,1,0:T(8,128)(2,1)S(1)}, u32[]{:S(2)}, u32[]{:S(2)}) %collective-permute-start.2) | collective-permute-done | bytes 393248 | tf_op jit(solution)/shard_map/ppermute | solution.py:51
  89.6 6.5 %collective-permute-start.3 = (bf16[4,48,1024]{2,1,0:T(8,128)(2,1)S(1)}, bf16[4,48,1024]{2,1,0:T(8,128)(2,1)}, u32[]{:S(2)}, u32[]{:S(2)}) collective-permute-start(bf16[4,48,1024]{2,1,0:T(8,128)(2,1)S(1)} %get-tuple-element.51.refs_0_), channel_id=1, source_target_pairs={{0,2},{1,3},{2,0},{3,1},{64,66},{65,67},{66,64},{67,65},{128,130},... | collective-permute-start | bytes 1179656 | tf_op jit(solution)/shard_map/ppermute | solution.py:51
  96.1 3.1 %shuffle.3 = (bf16[4,48,1024]{2,1,0:T(8,128)(2,1)S(1)}, bf16[4,48,1024]{2,1,0:T(8,128)(2,1)S(1)}, bf16[4,48,1024]{2,1,0:T(8,128)(2,1)S(1)}, bf16[4,48,1024]{2,1,0:T(8,128)(2,1)S(1)}) custom-call(bf16[768,1024]{1,0:T(8,128)(2,1)} %bitcast.7.rows_ref), custom_call_target="tpu_custom_call" | custom-call | flops 1207959552 | bytes 3145728 | tf_op jit(solution)/shard_map/shuffle/pallas_call | solution.py:193
  99.2 5.5 %collective-permute-done.3.refs_4_ = bf16[4,48,1024]{2,1,0:T(8,128)(2,1)} collective-permute-done((bf16[4,48,1024]{2,1,0:T(8,128)(2,1)S(1)}, bf16[4,48,1024]{2,1,0:T(8,128)(2,1)}, u32[]{:S(2)}, u32[]{:S(2)}) %collective-permute-start.3) | collective-permute-done | bytes 393248 | tf_op jit(solution)/shard_map/ppermute | solution.py:51
  104.6 1.7 collective-permute-start.4
  106.7 1.7 collective-permute-start.5
  108.4 8.3 %collective-permute-done.4.refs_5_ = bf16[4,48,1024]{2,1,0:T(8,128)(2,1)S(1)} collective-permute-done((bf16[4,48,1024]{2,1,0:T(8,128)(2,1)S(1)}, bf16[4,48,1024]{2,1,0:T(8,128)(2,1)S(1)}, u32[]{:S(2)}, u32[]{:S(2)}) %collective-permute-start.4) | collective-permute-done | bytes 393248 | tf_op jit(solution)/shard_map/ppermute | solution.py:51
  116.7 1.8 collective-permute-start.16
  118.5 8.1 %collective-permute-done.6.refs_7_ = bf16[4,48,1024]{2,1,0:T(8,128)(2,1)S(1)} collective-permute-done((bf16[4,48,1024]{2,1,0:T(8,128)(2,1)S(1)}, bf16[4,48,1024]{2,1,0:T(8,128)(2,1)S(1)}, u32[]{:S(2)}, u32[]{:S(2)}) %collective-permute-start.6) | collective-permute-done | bytes 393248 | tf_op jit(solution)/shard_map/ppermute | solution.py:51
  127.1 12.9 %collective-permute-done.5.refs_6_ = bf16[4,48,1024]{2,1,0:T(8,128)(2,1)S(1)} collective-permute-done((bf16[4,48,1024]{2,1,0:T(8,128)(2,1)S(1)}, bf16[4,48,1024]{2,1,0:T(8,128)(2,1)S(1)}, u32[]{:S(2)}, u32[]{:S(2)}) %collective-permute-start.5) | collective-permute-done | bytes 393248 | tf_op jit(solution)/shard_map/ppermute | solution.py:51
  141.1 5.8 %hidden.1 = (bf16[192,512]{1,0:T(8,128)(2,1)S(1)}, bf16[192,512]{1,0:T(8,128)(2,1)S(1)}, f32[384,1024]{1,0:T(8,128)S(1)}) custom-call(bf16[4,48,1024]{2,1,0:T(8,128)(2,1)S(1)} %get-tuple-element.51.refs_0_, bf16[4,48,1024]{2,1,0:T(8,128)(2,1)S(1)} %collective-permute-done.refs_1_, bf16[4,48,1024]{2,1,0:T(8,128)(2,1)S(1)} %collective-permute-done.1.refs_2_, ...), custom_call_target="tpu_custom_call" | custom-call | flops 3221225472 | bytes 16777216 | tf_op jit(solution)/shard_map/hidden/pallas_call | solution.py:252
  148.3 2.1 collective-permute-done.16.refs_1_
  150.7 6.7 %collective-permute-done.18.refs_3_ = bf16[4,48,1024]{2,1,0:T(8,128)(2,1)S(1)} collective-permute-done((bf16[4,48,1024]{2,1,0:T(8,128)(2,1)S(1)}, bf16[4,48,1024]{2,1,0:T(8,128)(2,1)S(1)}, u32[]{:S(2)}, u32[]{:S(2)}) %collective-permute-start.18) | collective-permute-done | bytes 393248 | tf_op jit(solution)/shard_map/ppermute | solution.py:51
  157.3 6.3 %d_hidden.1 = (f32[192,512]{1,0:T(8,128)S(1)}, bf16[192,512]{1,0:T(8,128)(2,1)S(1)}) custom-call(bf16[4,48,1024]{2,1,0:T(8,128)(2,1)S(1)} %get-tuple-element.68.refs_0_, bf16[4,48,1024]{2,1,0:T(8,128)(2,1)S(1)} %collective-permute-done.16.refs_1_, bf16[4,48,1024]{2,1,0:T(8,128)(2,1)S(1)} %collective-permute-done.17.refs_2_, ...), custom_call_target="tpu_custom_call" | custom-call | flops 1610612736 | bytes 12582912 | tf_op jit(solution)/shard_map/d_hidden/pallas_call | solution.py:278
  163.7 2.5 collective-permute-start.19
  166.1 5.3 %expert_out.1 = (bf16[4,48,1024]{2,1,0:T(8,128)(2,1)S(1)}, bf16[4,48,1024]{2,1,0:T(8,128)(2,1)S(1)}, bf16[4,48,1024]{2,1,0:T(8,128)(2,1)S(1)}, bf16[4,48,1024]{2,1,0:T(8,128)(2,1)S(1)}) custom-call(bf16[192,512]{1,0:T(8,128)(2,1)S(1)} %get-tuple-element.61.near, bf16[192,512]{1,0:T(8,128)(2,1)S(1)} %collective-permute-done.9.other, ...), custom_call_target="tpu_custom_call" | custom-call | flops 1610612736 | bytes 10485760 | tf_op jit(solution)/shard_map/expert_out/pallas_call | solution.py:317
  171.9 4.1 %collective-permute-start.14 = (bf16[4,48,1024]{2,1,0:T(8,128)(2,1)S(1)}, bf16[4,48,1024]{2,1,0:T(8,128)(2,1)S(1)}, u32[]{:S(2)}, u32[]{:S(2)}) collective-permute-start(bf16[4,48,1024]{2,1,0:T(8,128)(2,1)S(1)} %get-tuple-element.65), channel_id=1, source_target_pairs={{130,0},{131,1},{128,2},{129,3},{194,64},{195,65},{192,66},{193,67... | collective-permute-start | bytes 1179656 | tf_op jit(solution)/shard_map/ppermute | solution.py:51
  177.1 5.8 %expert_grad.3 = (bf16[4,48,1024]{2,1,0:T(8,128)(2,1)S(1)}, bf16[4,48,1024]{2,1,0:T(8,128)(2,1)}, bf16[4,48,1024]{2,1,0:T(8,128)(2,1)S(1)}, bf16[4,48,1024]{2,1,0:T(8,128)(2,1)S(1)}) custom-call(f32[384,1024]{1,0:T(8,128)S(1)} %get-tuple-element.67.acts, bf16[192,512]{1,0:T(8,128)(2,1)S(1)} %collective-permute-done.19.dh, bf16[4096,256]{1,0:T(8,128)(2,1)S(1)} %bitcast.17, ...), custom_call_target="tpu_custom_call" | custom-call | flops 1610612736 | bytes 12582912 | tf_op jit(solution)/shard_map/expert_grad/pallas_call | solution.py:356
  182.9 7.8 %collective-permute-done.13.b1 = bf16[4,48,1024]{2,1,0:T(8,128)(2,1)S(1)} collective-permute-done((bf16[4,48,1024]{2,1,0:T(8,128)(2,1)S(1)}, bf16[4,48,1024]{2,1,0:T(8,128)(2,1)S(1)}, u32[]{:S(2)}, u32[]{:S(2)}) %collective-permute-start.13) | collective-permute-done | bytes 393248 | tf_op jit(solution)/shard_map/ppermute | solution.py:51
  190.7 12.0 %collective-permute-done.14.b2 = bf16[4,48,1024]{2,1,0:T(8,128)(2,1)S(1)} collective-permute-done((bf16[4,48,1024]{2,1,0:T(8,128)(2,1)S(1)}, bf16[4,48,1024]{2,1,0:T(8,128)(2,1)S(1)}, u32[]{:S(2)}, u32[]{:S(2)}) %collective-permute-start.14) | collective-permute-done | bytes 393248 | tf_op jit(solution)/shard_map/ppermute | solution.py:51
  202.7 2.6 collective-permute-done.15.b3
  205.3 1.5 unshuffle.2
  208.0 6.9 %all-to-all-start.2 = ((bf16[16,48,1024]{2,1,0:T(8,128)(2,1)}), bf16[16,48,1024]{2,1,0:T(8,128)(2,1)}, u32[]{:S(2)}, u32[]{:S(2)}) async-start(bf16[16,48,1024]{2,1,0:T(8,128)(2,1)} %bitcast.23), calls=%async_computation.2 | async-start | bytes 3145728 | tf_op jit(solution)/shard_map/all_to_all | solution.py:55
  214.9 3.0 %collective-permute-start.23 = (bf16[4,48,1024]{2,1,0:T(8,128)(2,1)}, bf16[4,48,1024]{2,1,0:T(8,128)(2,1)S(1)}, u32[]{:S(2)}, u32[]{:S(2)}) collective-permute-start(bf16[4,48,1024]{2,1,0:T(8,128)(2,1)} %copy-done.18), channel_id=1, source_target_pairs={{0,2},{1,3},{2,0},{3,1},{64,66},{65,67},{66,64},{67,65},{128,130},... | collective-permute-start | bytes 1179656 | tf_op jit(solution)/shard_map/ppermute | solution.py:51
  217.9 1.6 copy-done.2
  219.5 1.4 copy-done.4
  220.9 5.1 %expert_grad.2 = (bf16[4,48,1024]{2,1,0:T(8,128)(2,1)S(1)}, bf16[4,48,1024]{2,1,0:T(8,128)(2,1)S(1)}, bf16[4,48,1024]{2,1,0:T(8,128)(2,1)S(1)}, bf16[4,48,1024]{2,1,0:T(8,128)(2,1)S(1)}) custom-call(f32[384,1024]{1,0:T(8,128)S(1)} %copy-done.4, f32[192,512]{1,0:T(8,128)S(1)} %get-tuple-element.72.dh, bf16[4096,256]{1,0:T(8,128)(2,1)S(1)} %bitcast.18, ...), custom_call_target="tpu_custom_call" | custom-call | flops 1610612736 | bytes 12582912 | tf_op jit(solution)/shard_map/expert_grad/pallas_call | solution.py:356
  226.1 2.0 collective-permute-start.25
  229.8 4.1 %collective-permute-start.24 = (bf16[4,48,1024]{2,1,0:T(8,128)(2,1)S(1)}, bf16[4,48,1024]{2,1,0:T(8,128)(2,1)S(1)}, u32[]{:S(2)}, u32[]{:S(2)}) collective-permute-start(bf16[4,48,1024]{2,1,0:T(8,128)(2,1)S(1)} %add_convert_fusion.1), channel_id=1, source_target_pairs={{130,0},{131,1},{128,2},{129,3},{194,64},{195,65},{192,66},{193,67... | collective-permute-start | bytes 1179656 | tf_op jit(solution)/shard_map/ppermute | solution.py:51
  233.9 24.8 %collective-permute-done.25 = bf16[4,48,1024]{2,1,0:T(8,128)(2,1)S(1)} collective-permute-done((bf16[4,48,1024]{2,1,0:T(8,128)(2,1)S(1)}, bf16[4,48,1024]{2,1,0:T(8,128)(2,1)S(1)}, u32[]{:S(2)}, u32[]{:S(2)}) %collective-permute-start.25) | collective-permute-done | bytes 393248 | tf_op jit(solution)/shard_map/ppermute | solution.py:51
  259.7 7.0 %collective-permute-done.26.b3 = bf16[4,48,1024]{2,1,0:T(8,128)(2,1)S(1)} collective-permute-done((bf16[4,48,1024]{2,1,0:T(8,128)(2,1)S(1)}, bf16[4,48,1024]{2,1,0:T(8,128)(2,1)S(1)}, u32[]{:S(2)}, u32[]{:S(2)}) %collective-permute-start.26) | collective-permute-done | bytes 393248 | tf_op jit(solution)/shard_map/ppermute | solution.py:51
  266.7 2.7 unshuffle.3
  269.4 6.8 %all-to-all-start.3 = ((bf16[16,48,1024]{2,1,0:T(8,128)(2,1)}), bf16[16,48,1024]{2,1,0:T(8,128)(2,1)S(1)}, u32[]{:S(2)}, u32[]{:S(2)}) async-start(bf16[16,48,1024]{2,1,0:T(8,128)(2,1)} %bitcast.13), calls=%async_computation.3 | async-start | bytes 3145728 | tf_op jit(solution)/shard_map/all_to_all | solution.py:55
  276.4 3.6 %combine.2 = bf16[128,4096]{1,0:T(8,128)(2,1)} custom-call(s32[2]{0:T(128)S(1)} %pad_add_fusion.where, s32[1,128]{1,0:T(1,128)S(1)} %bitcast.31, s32[128,1]{1,0:T(8,128)S(1)} %copy.19.ids_col, s32[128,1]{1,0:T(8,128)S(1)} %copy.20.level_col, bf16[768,1024]{1,0:T(8,128)(2,1)} %bitcast.12.back_ref), custom_call_target="tpu_custom_call" | custom-call | flops 805306368 | bytes 3145728 | tf_op jit(solution)/shard_map/combine/pallas_call | solution.py:142
  280.0 15.6 %all-to-all-done.3 = bf16[16,48,1024]{2,1,0:T(8,128)(2,1)S(1)} async-done(((bf16[16,48,1024]{2,1,0:T(8,128)(2,1)}), bf16[16,48,1024]{2,1,0:T(8,128)(2,1)S(1)}, u32[]{:S(2)}, u32[]{:S(2)}) %all-to-all-start.3) | async-done | bytes 1572896 | tf_op jit(solution)/shard_map/all_to_all | solution.py:55
  295.5 2.7 combine.3
  (77 shorter events, 19.1 us)
Async XLA Ops:
  0.6 51.6 %collective-permute-start.11 = (bf16[256,4096]{1,0:T(8,128)(2,1)}, bf16[256,4096]{1,0:T(8,128)(2,1)}, u32[]{:S(2)}, u32[]{:S(2)}) collective-permute-start(bf16[256,4096]{1,0:T(8,128)(2,1)} %bitcast.10.wd0.refs_4_), channel_id=1, source_target_pairs={{0,2},{1,3},{2,0},{3,1},{64,66},{65,67},{66,64},{67,65},{128,130},... | collective-permute-start | bytes 6291464 | tf_op jit(solution)/shard_map/ppermute | solution.py:51
  4.7 1.2 copy-start.12
  7.6 1.2 copy-start.7
  8.8 5.7 %copy-start = (bf16[1,4096,256]{2,1,0:T(8,128)(2,1)S(1)}, bf16[1,4096,256]{2,1,0:T(8,128)(2,1)}, u32[]{:S(2)}) copy-start(bf16[1,4096,256]{2,1,0:T(8,128)(2,1)} %param.15) | copy-start | bytes 6291460
  8.8 6.3 %copy-start.14 = (bf16[128,2048]{1,0:T(8,128)(2,1)S(1)}, bf16[128,2048]{1,0:T(8,128)(2,1)}, u32[]{:S(2)}) copy-start(bf16[128,2048]{1,0:T(8,128)(2,1)} %q_ref.1) | copy-start | bytes 1572868
  8.8 6.3 %copy-start.19 = (bf16[128,128]{1,0:T(8,128)(2,1)S(1)}, bf16[128,128]{1,0:T(8,128)(2,1)}, u32[]{:S(2)}) copy-start(bf16[128,128]{1,0:T(8,128)(2,1)} %k_ref.1) | copy-start | bytes 98308
  8.8 6.3 %copy-start.20 = (bf16[128,128]{1,0:T(8,128)(2,1)S(1)}, bf16[128,128]{1,0:T(8,128)(2,1)}, u32[]{:S(2)}) copy-start(bf16[128,128]{1,0:T(8,128)(2,1)} %v_ref.1) | copy-start | bytes 98308
  8.8 30.0 %all-to-all-start = ((bf16[16,48,1024]{2,1,0:T(8,128)(2,1)}), bf16[16,48,1024]{2,1,0:T(8,128)(2,1)}, u32[]{:S(2)}, u32[]{:S(2)}) async-start(bf16[16,48,1024]{2,1,0:T(8,128)(2,1)} %bitcast.25), calls=%async_computation | async-start | bytes 3145728 | tf_op jit(solution)/shard_map/all_to_all | solution.py:55
  14.4 13.0 %copy-start.9 = (s32[128,1]{0,1:T(1,128)S(1)}, s32[128,1]{0,1:T(1,128)}, u32[]{:S(2)}) copy-start(s32[128,1]{0,1:T(1,128)} %param.14) | copy-start | bytes 1540
  14.5 13.0 %copy-start.11 = (s32[128,1]{0,1:T(1,128)S(1)}, s32[128,1]{0,1:T(1,128)}, u32[]{:S(2)}) copy-start(s32[128,1]{0,1:T(1,128)} %param.13) | copy-start | bytes 1540
  14.5 13.0 %copy-start.13 = (bf16[128,4096]{1,0:T(8,128)(2,1)S(1)}, bf16[128,4096]{1,0:T(8,128)(2,1)}, u32[]{:S(2)}) copy-start(bf16[128,4096]{1,0:T(8,128)(2,1)} %x_ref.3) | copy-start | bytes 3145732
  14.5 91.9 %collective-permute-start.7 = (bf16[4096,256]{1,0:T(8,128)(2,1)S(1)}, bf16[4096,256]{1,0:T(8,128)(2,1)}, u32[]{:S(2)}, u32[]{:S(2)}) collective-permute-start(bf16[4096,256]{1,0:T(8,128)(2,1)S(1)} %bitcast.15), channel_id=1, source_target_pairs={{0,1},{1,0},{2,3},{3,2},{64,65},{65,64},{66,67},{67,66},{128,129},... | collective-permute-start | bytes 6291464 | tf_op jit(solution)/shard_map/ppermute | solution.py:51
  14.6 92.1 %collective-permute-start.8 = (bf16[4096,256]{1,0:T(8,128)(2,1)}, bf16[4096,256]{1,0:T(8,128)(2,1)}, u32[]{:S(2)}, u32[]{:S(2)}) collective-permute-start(bf16[4096,256]{1,0:T(8,128)(2,1)} %bitcast.19), channel_id=1, source_target_pairs={{0,1},{1,0},{2,3},{3,2},{64,65},{65,64},{66,67},{67,66},{128,129},... | collective-permute-start | bytes 6291464 | tf_op jit(solution)/shard_map/ppermute | solution.py:51
  29.2 1.2 copy-start.6
  38.9 57.2 %all-to-all-start.1 = ((bf16[16,48,1024]{2,1,0:T(8,128)(2,1)}), bf16[16,48,1024]{2,1,0:T(8,128)(2,1)}, u32[]{:S(2)}, u32[]{:S(2)}) async-start(bf16[16,48,1024]{2,1,0:T(8,128)(2,1)} %bitcast.24), calls=%async_computation.1 | async-start | bytes 3145728 | tf_op jit(solution)/shard_map/all_to_all | solution.py:55
  46.2 12.9 %collective-permute-start = (bf16[4,48,1024]{2,1,0:T(8,128)(2,1)S(1)}, bf16[4,48,1024]{2,1,0:T(8,128)(2,1)S(1)}, u32[]{:S(2)}, u32[]{:S(2)}) collective-permute-start(bf16[4,48,1024]{2,1,0:T(8,128)(2,1)S(1)} %get-tuple-element.52), channel_id=1, source_target_pairs={{0,64},{1,65},{2,194},{3,195},{64,128},{65,129},{66,2},{67,3},{128... | collective-permute-start | bytes 1179656 | tf_op jit(solution)/shard_map/ppermute | solution.py:51
  52.2 94.7 %collective-permute-start.10 = (bf16[256,4096]{1,0:T(8,128)(2,1)}, bf16[256,4096]{1,0:T(8,128)(2,1)}, u32[]{:S(2)}, u32[]{:S(2)}) collective-permute-start(bf16[256,4096]{1,0:T(8,128)(2,1)} %bitcast.10.wd0.refs_4_), channel_id=1, source_target_pairs={{0,1},{1,0},{2,3},{3,2},{64,65},{65,64},{66,67},{67,66},{128,129},... | collective-permute-start | bytes 6291464 | tf_op jit(solution)/shard_map/ppermute | solution.py:51
  52.2 105.2 %collective-permute-start.12 = (bf16[256,4096]{1,0:T(8,128)(2,1)}, bf16[256,4096]{1,0:T(8,128)(2,1)}, u32[]{:S(2)}, u32[]{:S(2)}) collective-permute-start(bf16[256,4096]{1,0:T(8,128)(2,1)} %collective-permute-done.11.wd2.refs_6_), channel_id=1, source_target_pairs={{0,1},{1,0},{2,3},{3,2},{64,65},{65,64},{66,67},{67,66},{128,129},... | collective-permute-start | bytes 6291464 | tf_op jit(solution)/shard_map/ppermute | solution.py:51
  59.0 18.8 %collective-permute-start.1 = (bf16[4,48,1024]{2,1,0:T(8,128)(2,1)S(1)}, bf16[4,48,1024]{2,1,0:T(8,128)(2,1)S(1)}, u32[]{:S(2)}, u32[]{:S(2)}) collective-permute-start(bf16[4,48,1024]{2,1,0:T(8,128)(2,1)S(1)} %get-tuple-element.53), channel_id=1, source_target_pairs={{0,130},{1,131},{2,128},{3,129},{64,194},{65,195},{66,192},{67,193... | collective-permute-start | bytes 1179656 | tf_op jit(solution)/shard_map/ppermute | solution.py:51
  77.8 11.0 %collective-permute-start.2 = (bf16[4,48,1024]{2,1,0:T(8,128)(2,1)S(1)}, bf16[4,48,1024]{2,1,0:T(8,128)(2,1)S(1)}, u32[]{:S(2)}, u32[]{:S(2)}) collective-permute-start(bf16[4,48,1024]{2,1,0:T(8,128)(2,1)S(1)} %get-tuple-element.60), channel_id=1, source_target_pairs={{0,194},{1,195},{2,64},{3,65},{64,2},{65,3},{66,128},{67,129},{128... | collective-permute-start | bytes 1179656 | tf_op jit(solution)/shard_map/ppermute | solution.py:51
  89.6 15.0 %collective-permute-start.3 = (bf16[4,48,1024]{2,1,0:T(8,128)(2,1)S(1)}, bf16[4,48,1024]{2,1,0:T(8,128)(2,1)}, u32[]{:S(2)}, u32[]{:S(2)}) collective-permute-start(bf16[4,48,1024]{2,1,0:T(8,128)(2,1)S(1)} %get-tuple-element.51.refs_0_), channel_id=1, source_target_pairs={{0,2},{1,3},{2,0},{3,1},{64,66},{65,67},{66,64},{67,65},{128,130},... | collective-permute-start | bytes 1179656 | tf_op jit(solution)/shard_map/ppermute | solution.py:51
  96.1 10.3 %copy-start.17 = (bf16[4,48,1024]{2,1,0:T(8,128)(2,1)S(1)}, bf16[4,48,1024]{2,1,0:T(8,128)(2,1)}, u32[]{:S(2)}) copy-start(bf16[4,48,1024]{2,1,0:T(8,128)(2,1)} %copy-done.16) | copy-start | bytes 1179652
  96.1 45.0 %copy-start.1 = (bf16[1,4096,256]{2,1,0:T(8,128)(2,1)S(1)}, bf16[1,4096,256]{2,1,0:T(8,128)(2,1)}, u32[]{:S(2)}) copy-start(bf16[1,4096,256]{2,1,0:T(8,128)(2,1)} %param.16) | copy-start | bytes 6291460
  104.6 12.1 %collective-permute-start.4 = (bf16[4,48,1024]{2,1,0:T(8,128)(2,1)S(1)}, bf16[4,48,1024]{2,1,0:T(8,128)(2,1)S(1)}, u32[]{:S(2)}, u32[]{:S(2)}) collective-permute-start(bf16[4,48,1024]{2,1,0:T(8,128)(2,1)S(1)} %collective-permute-done.refs_1_), channel_id=1, source_target_pairs={{0,2},{1,3},{2,0},{3,1},{64,66},{65,67},{66,64},{67,65},{128,130},... | collective-permute-start | bytes 1179656 | tf_op jit(solution)/shard_map/ppermute | solution.py:51
  106.4 20.2 %collective-permute-start.6 = (bf16[4,48,1024]{2,1,0:T(8,128)(2,1)S(1)}, bf16[4,48,1024]{2,1,0:T(8,128)(2,1)S(1)}, u32[]{:S(2)}, u32[]{:S(2)}) collective-permute-start(bf16[4,48,1024]{2,1,0:T(8,128)(2,1)S(1)} %copy-done.17), channel_id=1, source_target_pairs={{0,2},{1,3},{2,0},{3,1},{64,66},{65,67},{66,64},{67,65},{128,130},... | collective-permute-start | bytes 1179656 | tf_op jit(solution)/shard_map/ppermute | solution.py:51
  106.7 33.3 %collective-permute-start.5 = (bf16[4,48,1024]{2,1,0:T(8,128)(2,1)S(1)}, bf16[4,48,1024]{2,1,0:T(8,128)(2,1)S(1)}, u32[]{:S(2)}, u32[]{:S(2)}) collective-permute-start(bf16[4,48,1024]{2,1,0:T(8,128)(2,1)S(1)} %collective-permute-done.1.refs_2_), channel_id=1, source_target_pairs={{0,2},{1,3},{2,0},{3,1},{64,66},{65,67},{66,64},{67,65},{128,130},... | collective-permute-start | bytes 1179656 | tf_op jit(solution)/shard_map/ppermute | solution.py:51
  116.7 33.7 %collective-permute-start.16 = (bf16[4,48,1024]{2,1,0:T(8,128)(2,1)S(1)}, bf16[4,48,1024]{2,1,0:T(8,128)(2,1)S(1)}, u32[]{:S(2)}, u32[]{:S(2)}) collective-permute-start(bf16[4,48,1024]{2,1,0:T(8,128)(2,1)S(1)} %get-tuple-element.69), channel_id=1, source_target_pairs={{0,64},{1,65},{2,194},{3,195},{64,128},{65,129},{66,2},{67,3},{128... | collective-permute-start | bytes 1179656 | tf_op jit(solution)/shard_map/ppermute | solution.py:51
  126.6 24.0 %collective-permute-start.17 = (bf16[4,48,1024]{2,1,0:T(8,128)(2,1)S(1)}, bf16[4,48,1024]{2,1,0:T(8,128)(2,1)S(1)}, u32[]{:S(2)}, u32[]{:S(2)}) collective-permute-start(bf16[4,48,1024]{2,1,0:T(8,128)(2,1)S(1)} %get-tuple-element.70), channel_id=1, source_target_pairs={{0,130},{1,131},{2,128},{3,129},{64,194},{65,195},{66,192},{67,193... | collective-permute-start | bytes 1179656 | tf_op jit(solution)/shard_map/ppermute | solution.py:51
  140.0 17.3 %collective-permute-start.18 = (bf16[4,48,1024]{2,1,0:T(8,128)(2,1)S(1)}, bf16[4,48,1024]{2,1,0:T(8,128)(2,1)S(1)}, u32[]{:S(2)}, u32[]{:S(2)}) collective-permute-start(bf16[4,48,1024]{2,1,0:T(8,128)(2,1)S(1)} %get-tuple-element.71), channel_id=1, source_target_pairs={{0,194},{1,195},{2,64},{3,65},{64,2},{65,3},{66,128},{67,129},{128... | collective-permute-start | bytes 1179656 | tf_op jit(solution)/shard_map/ppermute | solution.py:51
  146.9 30.3 %copy-start.3 = (f32[384,1024]{1,0:T(8,128)}, f32[384,1024]{1,0:T(8,128)S(1)}, u32[]{:S(2)}) copy-start(f32[384,1024]{1,0:T(8,128)S(1)} %get-tuple-element.67.acts) | copy-start | bytes 4718596
  146.9 19.3 %collective-permute-start.9 = (bf16[192,512]{1,0:T(8,128)(2,1)S(1)}, bf16[192,512]{1,0:T(8,128)(2,1)S(1)}, u32[]{:S(2)}, u32[]{:S(2)}) collective-permute-start(bf16[192,512]{1,0:T(8,128)(2,1)S(1)} %get-tuple-element.62), channel_id=1, source_target_pairs={{0,2},{1,3},{2,0},{3,1},{64,66},{65,67},{66,64},{67,65},{128,130},... | collective-permute-start | bytes 589832 | tf_op jit(solution)/shard_map/ppermute | solution.py:51
  163.7 13.4 %collective-permute-start.19 = (bf16[192,512]{1,0:T(8,128)(2,1)S(1)}, bf16[192,512]{1,0:T(8,128)(2,1)S(1)}, u32[]{:S(2)}, u32[]{:S(2)}) collective-permute-start(bf16[192,512]{1,0:T(8,128)(2,1)S(1)} %get-tuple-element.74), channel_id=1, source_target_pairs={{0,2},{1,3},{2,0},{3,1},{64,66},{65,67},{66,64},{67,65},{128,130},... | collective-permute-start | bytes 589832 | tf_op jit(solution)/shard_map/ppermute | solution.py:51
  171.4 19.3 %collective-permute-start.13 = (bf16[4,48,1024]{2,1,0:T(8,128)(2,1)S(1)}, bf16[4,48,1024]{2,1,0:T(8,128)(2,1)S(1)}, u32[]{:S(2)}, u32[]{:S(2)}) collective-permute-start(bf16[4,48,1024]{2,1,0:T(8,128)(2,1)S(1)} %get-tuple-element.64), channel_id=1, source_target_pairs={{64,0},{65,1},{194,2},{195,3},{128,64},{129,65},{2,66},{3,67},{192... | collective-permute-start | bytes 1179656 | tf_op jit(solution)/shard_map/ppermute | solution.py:51
  171.9 30.8 %collective-permute-start.14 = (bf16[4,48,1024]{2,1,0:T(8,128)(2,1)S(1)}, bf16[4,48,1024]{2,1,0:T(8,128)(2,1)S(1)}, u32[]{:S(2)}, u32[]{:S(2)}) collective-permute-start(bf16[4,48,1024]{2,1,0:T(8,128)(2,1)S(1)} %get-tuple-element.65), channel_id=1, source_target_pairs={{130,0},{131,1},{128,2},{129,3},{194,64},{195,65},{192,66},{193,67... | collective-permute-start | bytes 1179656 | tf_op jit(solution)/shard_map/ppermute | solution.py:51
  176.1 29.2 %collective-permute-start.15 = (bf16[4,48,1024]{2,1,0:T(8,128)(2,1)S(1)}, bf16[4,48,1024]{2,1,0:T(8,128)(2,1)S(1)}, u32[]{:S(2)}, u32[]{:S(2)}) collective-permute-start(bf16[4,48,1024]{2,1,0:T(8,128)(2,1)S(1)} %get-tuple-element.66), channel_id=1, source_target_pairs={{194,0},{195,1},{64,2},{65,3},{2,64},{3,65},{128,66},{129,67},{66,... | collective-permute-start | bytes 1179656 | tf_op jit(solution)/shard_map/ppermute | solution.py:51
  182.9 23.9 %copy-start.18 = (bf16[4,48,1024]{2,1,0:T(8,128)(2,1)}, bf16[4,48,1024]{2,1,0:T(8,128)(2,1)S(1)}, u32[]{:S(2)}) copy-start(bf16[4,48,1024]{2,1,0:T(8,128)(2,1)S(1)} %get-tuple-element.79) | copy-start | bytes 1179652
  182.9 45.2 %collective-permute-start.21 = (bf16[4,48,1024]{2,1,0:T(8,128)(2,1)}, bf16[4,48,1024]{2,1,0:T(8,128)(2,1)}, u32[]{:S(2)}, u32[]{:S(2)}) collective-permute-start(bf16[4,48,1024]{2,1,0:T(8,128)(2,1)} %get-tuple-element.77), channel_id=1, source_target_pairs={{0,2},{1,3},{2,0},{3,1},{64,66},{65,67},{66,64},{67,65},{128,130},... | collective-permute-start | bytes 1179656 | tf_op jit(solution)/shard_map/ppermute | solution.py:51
  206.8 1.1 copy-start.5
  208.0 61.5 %all-to-all-start.2 = ((bf16[16,48,1024]{2,1,0:T(8,128)(2,1)}), bf16[16,48,1024]{2,1,0:T(8,128)(2,1)}, u32[]{:S(2)}, u32[]{:S(2)}) async-start(bf16[16,48,1024]{2,1,0:T(8,128)(2,1)} %bitcast.23), calls=%async_computation.2 | async-start | bytes 3145728 | tf_op jit(solution)/shard_map/all_to_all | solution.py:55
  214.9 14.8 %collective-permute-start.23 = (bf16[4,48,1024]{2,1,0:T(8,128)(2,1)}, bf16[4,48,1024]{2,1,0:T(8,128)(2,1)S(1)}, u32[]{:S(2)}, u32[]{:S(2)}) collective-permute-start(bf16[4,48,1024]{2,1,0:T(8,128)(2,1)} %copy-done.18), channel_id=1, source_target_pairs={{0,2},{1,3},{2,0},{3,1},{64,66},{65,67},{66,64},{67,65},{128,130},... | collective-permute-start | bytes 1179656 | tf_op jit(solution)/shard_map/ppermute | solution.py:51
  217.9 1.6 copy-start.2
  219.5 1.4 copy-start.4
  226.0 33.6 %collective-permute-start.20 = (bf16[4,48,1024]{2,1,0:T(8,128)(2,1)S(1)}, bf16[4,48,1024]{2,1,0:T(8,128)(2,1)S(1)}, u32[]{:S(2)}, u32[]{:S(2)}) collective-permute-start(bf16[4,48,1024]{2,1,0:T(8,128)(2,1)S(1)} %get-tuple-element.75), channel_id=1, source_target_pairs={{0,2},{1,3},{2,0},{3,1},{64,66},{65,67},{66,64},{67,65},{128,130},... | collective-permute-start | bytes 1179656 | tf_op jit(solution)/shard_map/ppermute | solution.py:51
  226.1 32.7 %collective-permute-start.25 = (bf16[4,48,1024]{2,1,0:T(8,128)(2,1)S(1)}, bf16[4,48,1024]{2,1,0:T(8,128)(2,1)S(1)}, u32[]{:S(2)}, u32[]{:S(2)}) collective-permute-start(bf16[4,48,1024]{2,1,0:T(8,128)(2,1)S(1)} %get-tuple-element.81), channel_id=1, source_target_pairs={{0,2},{1,3},{2,0},{3,1},{64,66},{65,67},{66,64},{67,65},{128,130},... | collective-permute-start | bytes 1179656 | tf_op jit(solution)/shard_map/ppermute | solution.py:51
  229.2 30.5 %collective-permute-start.22 = (bf16[4,48,1024]{2,1,0:T(8,128)(2,1)S(1)}, bf16[4,48,1024]{2,1,0:T(8,128)(2,1)S(1)}, u32[]{:S(2)}, u32[]{:S(2)}) collective-permute-start(bf16[4,48,1024]{2,1,0:T(8,128)(2,1)S(1)} %add_convert_fusion.2), channel_id=1, source_target_pairs={{64,0},{65,1},{194,2},{195,3},{128,64},{129,65},{2,66},{3,67},{192... | collective-permute-start | bytes 1179656 | tf_op jit(solution)/shard_map/ppermute | solution.py:51
  229.8 29.9 %collective-permute-start.24 = (bf16[4,48,1024]{2,1,0:T(8,128)(2,1)S(1)}, bf16[4,48,1024]{2,1,0:T(8,128)(2,1)S(1)}, u32[]{:S(2)}, u32[]{:S(2)}) collective-permute-start(bf16[4,48,1024]{2,1,0:T(8,128)(2,1)S(1)} %add_convert_fusion.1), channel_id=1, source_target_pairs={{130,0},{131,1},{128,2},{129,3},{194,64},{195,65},{192,66},{193,67... | collective-permute-start | bytes 1179656 | tf_op jit(solution)/shard_map/ppermute | solution.py:51
  258.9 7.9 %collective-permute-start.26 = (bf16[4,48,1024]{2,1,0:T(8,128)(2,1)S(1)}, bf16[4,48,1024]{2,1,0:T(8,128)(2,1)S(1)}, u32[]{:S(2)}, u32[]{:S(2)}) collective-permute-start(bf16[4,48,1024]{2,1,0:T(8,128)(2,1)S(1)} %add_convert_fusion), channel_id=1, source_target_pairs={{194,0},{195,1},{64,2},{65,3},{2,64},{3,65},{128,66},{129,67},{66,... | collective-permute-start | bytes 1179656 | tf_op jit(solution)/shard_map/ppermute | solution.py:51
  269.4 26.1 %all-to-all-start.3 = ((bf16[16,48,1024]{2,1,0:T(8,128)(2,1)}), bf16[16,48,1024]{2,1,0:T(8,128)(2,1)S(1)}, u32[]{:S(2)}, u32[]{:S(2)}) async-start(bf16[16,48,1024]{2,1,0:T(8,128)(2,1)} %bitcast.13), calls=%async_computation.3 | async-start | bytes 3145728 | tf_op jit(solution)/shard_map/all_to_all | solution.py:55
  (4 other events, 3.1 us)
